TPU v7x, 32 devices: a whole 2x2x4 slice. The times are simulated.
32 devices in a mesh: rep: 8 (over y, x, core), fsdp: 4 (over z).
Axes of the slice: x: 2, y: 2, z: 4, core: 2. Of those that a mesh axis runs over, the one named last changes fastest.
Arguments:
- hidden: bfloat16 [96, 2048, 768], P(('rep', 'fsdp')), may hold values from -6 to 6
- segments: int32 [96, 2048], P(('rep', 'fsdp')), may hold values from 0 to 5, never falling along the last dimension, each value on 1 to 682 neighbouring positions
- selected: int32 [96, 256], P(('rep', 'fsdp')), may hold values from 0 to 2047, as said below
- w_query: bfloat16 [768, 768], P('fsdp'), may hold values from -0.21875 to 0.21875
- w_key: bfloat16 [768, 768], P('fsdp'), may hold values from -0.21875 to 0.21875
- w_value: bfloat16 [768, 768], P('fsdp'), may hold values from -0.21875 to 0.21875
- w_out: bfloat16 [768, 768], P('fsdp'), may hold values from -0.875 to 0.875
- w_up: bfloat16 [768, 3072], P('fsdp'), may hold values from -0.21875 to 0.21875
- w_down: bfloat16 [3072, 768], P('fsdp'), may hold values from -0.109375 to 0.109375
- w_router: bfloat16 [768], P('fsdp'), may hold values from -0.21875 to 0.21875
- gain_attn: bfloat16 [768], P('fsdp'), may hold values from 0.099609375 to 1.8984375
- gain_mlp: bfloat16 [768], P('fsdp'), may hold values from 0.099609375 to 1.8984375
- cotangent: bfloat16 [96, 2048, 768], P(('rep', 'fsdp')), may hold values from -6 to 6
Outputs:
- out_hidden: bfloat16 [96, 2048, 768], P(('rep', 'fsdp'))
- grad_hidden: bfloat16 [96, 2048, 768], P(('rep', 'fsdp'))
- grad_query: float32 [768, 768], P('fsdp')
- grad_key: float32 [768, 768], P('fsdp')
- grad_value: float32 [768, 768], P('fsdp')
- grad_out: float32 [768, 768], P('fsdp')
- grad_up: float32 [768, 3072], P('fsdp')
- grad_down: float32 [3072, 768], P('fsdp')
- grad_router: float32 [768], P('fsdp')
- grad_gain_attn: float32 [768], P('fsdp')
- grad_gain_mlp: float32 [768], P('fsdp')
Inputs may be any that keep to these rules, and one draw needn't show every extreme that they name: `selected`: each row holds 256 distinct positions of its sequence in ascending order; 0 and 2047 are always among them.
All inputs are finite; a program needn't handle non-finite values.
Results may differ from a plain program's by a relative error of at most 0.015.
Values may be sent and summed in bfloat16 or wider, within the bound.
No kernel may reach another device: no remote copies, remote signals or barrier semaphores. Data moves between devices by JAX's collectives and lax.ppermute only.
A program may use at most 320 MiB of HBM per device.

v0:
```python
import jax
import jax.numpy as jnp
from jax import lax
from jax.sharding import PartitionSpec as P

HEADS = 12
HEAD_DIM = 64


EPSILON = 1e-06


def rms_scale(values):
    return lax.rsqrt(jnp.mean(values * values, axis=-1, keepdims=True) + EPSILON)


def norm_back(grad_normed, values, inverse, gain):
    scaled = grad_normed * gain
    grad_gain = jnp.sum(grad_normed * values * inverse, axis=(0, 1))
    grad_values = inverse * scaled - values * inverse * inverse * inverse * jnp.mean(
        scaled * values, axis=-1, keepdims=True
    )
    return (grad_values, grad_gain)


def mix_rows(left, right):
    return jnp.einsum("ska,ab->skb", left, right, preferred_element_type=jnp.float32)


def mix_back(left, right):
    return jnp.einsum("skb,ab->ska", left, right, preferred_element_type=jnp.float32)


def outer_sum(left, right):
    return jnp.einsum("ska,skb->ab", left, right, preferred_element_type=jnp.float32)


def place_rows(indicator, rows):
    width = rows.shape[-1]
    upper = rows.astype(jnp.bfloat16)
    remain = rows - upper.astype(jnp.float32)
    centre = remain.astype(jnp.bfloat16)
    lowest = (remain - centre.astype(jnp.float32)).astype(jnp.bfloat16)
    stacked = jnp.concatenate([upper, centre, lowest], axis=-1)
    placed = jnp.einsum("ezy,ezf->eyf", indicator, stacked, preferred_element_type=jnp.float32)
    return placed[..., :width] + placed[..., width : 2 * width] + placed[..., 2 * width :]


def on_device(
    hidden,
    segments,
    selected,
    w_query,
    w_key,
    w_value,
    w_out,
    w_up,
    w_down,
    w_router,
    gain_attn,
    gain_mlp,
    cotangent,
):
    (
        full_query,
        full_key,
        full_value,
        full_out,
        full_up,
        full_down,
        complete_router_weight,
        full_gain_attn,
        full_gain_mlp,
    ) = (
        lax.all_gather(w_query, "fsdp", axis=0, tiled=True),
        lax.all_gather(w_key, "fsdp", axis=0, tiled=True),
        lax.all_gather(w_value, "fsdp", axis=0, tiled=True),
        lax.all_gather(w_out, "fsdp", axis=0, tiled=True),
        lax.all_gather(w_up, "fsdp", axis=0, tiled=True),
        lax.all_gather(w_down, "fsdp", axis=0, tiled=True),
        lax.all_gather(w_router, "fsdp", axis=0, tiled=True),
        lax.all_gather(gain_attn, "fsdp", axis=0, tiled=True),
        lax.all_gather(gain_mlp, "fsdp", axis=0, tiled=True),
    )
    seq_count, length, width = hidden.shape
    keep_count = selected.shape[1]
    head_shape = (seq_count, keep_count, HEADS, HEAD_DIM)
    positions = lax.broadcasted_iota(jnp.int32, (seq_count, keep_count, length), 2)
    indicator_matrix = (selected[:, :, None] == positions).astype(jnp.bfloat16)
    router_scores = jnp.einsum(
        "zhe,e->zh", hidden, complete_router_weight, preferred_element_type=jnp.float32
    )
    routed_tokens = jnp.einsum(
        "ezy,eyf->ezf", indicator_matrix, hidden, preferred_element_type=jnp.float32
    )
    gating = jax.nn.sigmoid(jnp.take_along_axis(router_scores, selected, axis=1))
    inverse_attn = rms_scale(routed_tokens)
    normed = (routed_tokens * inverse_attn * full_gain_attn).astype(jnp.bfloat16)
    query_heads = mix_rows(normed, full_query).astype(jnp.bfloat16).reshape(head_shape)
    key_heads = mix_rows(normed, full_key).astype(jnp.bfloat16).reshape(head_shape)
    value_heads = mix_rows(normed, full_value).astype(jnp.bfloat16).reshape(head_shape)
    chosen_docs = jnp.take_along_axis(segments, selected, axis=1)
    allowed = (selected[:, :, None] >= selected[:, None, :]) & (
        chosen_docs[:, :, None] == chosen_docs[:, None, :]
    )

    def attention_scores(query_part, key_part):
        raw = (
            jnp.einsum("sqhe,skhe->shqk", query_part, key_part, preferred_element_type=jnp.float32)
            * 0.125
        )
        return jnp.where(allowed[:, None], raw, -1e30)

    scores = attention_scores(query_heads, key_heads)
    row_max = jnp.max(scores, axis=-1, keepdims=True)
    exponent = jnp.exp(scores - row_max)
    totals = jnp.sum(exponent, axis=-1, keepdims=True)
    log_total = row_max + jnp.log(totals)
    probs_low = (exponent / totals).astype(jnp.bfloat16)
    attended = jnp.einsum(
        "shqk,skhe->sqhe", probs_low, value_heads, preferred_element_type=jnp.float32
    )
    attended = attended.astype(jnp.bfloat16).reshape(seq_count, keep_count, width)
    attention_output = mix_rows(attended, full_out)
    middle = routed_tokens + attention_output
    inverse_mlp = rms_scale(middle)
    feedforward_normalized = (middle * inverse_mlp * full_gain_mlp).astype(jnp.bfloat16)
    before = mix_rows(feedforward_normalized, full_up)
    activated, gelu_back = jax.vjp(lambda inputs: jax.nn.gelu(inputs, approximate=False), before)
    activated_low = activated.astype(jnp.bfloat16)
    mlp_out = mix_rows(activated_low, full_down)
    delta = attention_output + mlp_out
    branch = gating[..., None] * delta
    out_hidden = (hidden.astype(jnp.float32) + place_rows(indicator_matrix, branch)).astype(
        jnp.bfloat16
    )
    (
        full_query,
        full_key,
        full_value,
        full_out,
        full_up,
        full_down,
        complete_router_weight,
        full_gain_attn,
        full_gain_mlp,
    ) = (
        lax.all_gather(w_query, "fsdp", axis=0, tiled=True),
        lax.all_gather(w_key, "fsdp", axis=0, tiled=True),
        lax.all_gather(w_value, "fsdp", axis=0, tiled=True),
        lax.all_gather(w_out, "fsdp", axis=0, tiled=True),
        lax.all_gather(w_up, "fsdp", axis=0, tiled=True),
        lax.all_gather(w_down, "fsdp", axis=0, tiled=True),
        lax.all_gather(w_router, "fsdp", axis=0, tiled=True),
        lax.all_gather(gain_attn, "fsdp", axis=0, tiled=True),
        lax.all_gather(gain_mlp, "fsdp", axis=0, tiled=True),
    )
    branch_gradient = jnp.einsum(
        "ezy,eyf->ezf", indicator_matrix, cotangent, preferred_element_type=jnp.float32
    )
    grad_gating = jnp.sum(branch_gradient * delta, axis=-1)
    grad_logit = grad_gating * gating * (1.0 - gating)
    grad_delta = branch_gradient * gating[..., None]
    grad_mlp_out = grad_delta.astype(jnp.bfloat16)
    grad_down_w = outer_sum(activated_low, grad_mlp_out)
    grad_activated = mix_back(grad_mlp_out, full_down)
    grad_before = gelu_back(grad_activated)[0].astype(jnp.bfloat16)
    up_weight_gradient = outer_sum(feedforward_normalized, grad_before)
    grad_normed_mlp = mix_back(grad_before, full_up)
    grad_middle, grad_gain_m = norm_back(grad_normed_mlp, middle, inverse_mlp, full_gain_mlp)
    grad_attn_out = (grad_delta + grad_middle).astype(jnp.bfloat16)
    grad_out_w = outer_sum(attended, grad_attn_out)
    grad_attended = mix_back(grad_attn_out, full_out).astype(jnp.bfloat16).reshape(head_shape)
    probabilities = jnp.exp(attention_scores(query_heads, key_heads) - log_total)
    grad_value_heads = jnp.einsum(
        "shqk,sqhe->skhe",
        probabilities.astype(jnp.bfloat16),
        grad_attended,
        preferred_element_type=jnp.float32,
    ).astype(jnp.bfloat16)
    grad_probs = jnp.einsum(
        "sqhe,skhe->shqk", grad_attended, value_heads, preferred_element_type=jnp.float32
    )
    grad_scores = probabilities * (
        grad_probs - jnp.sum(probabilities * grad_probs, axis=-1, keepdims=True)
    )
    grad_scores = jnp.where(allowed[:, None], grad_scores, 0.0).astype(jnp.bfloat16)
    grad_query_heads = (
        jnp.einsum("shqk,skhe->sqhe", grad_scores, key_heads, preferred_element_type=jnp.float32)
        * 0.125
    ).astype(jnp.bfloat16)
    grad_key_heads = (
        jnp.einsum("shqk,sqhe->skhe", grad_scores, query_heads, preferred_element_type=jnp.float32)
        * 0.125
    ).astype(jnp.bfloat16)
    flat_shape = (seq_count, keep_count, width)
    grad_queries = grad_query_heads.reshape(flat_shape)
    grad_keys = grad_key_heads.reshape(flat_shape)
    grad_values = grad_value_heads.reshape(flat_shape)
    grad_query_w = outer_sum(normed, grad_queries)
    grad_key_w = outer_sum(normed, grad_keys)
    grad_value_w = outer_sum(normed, grad_values)
    grad_normed = (
        mix_back(grad_queries, full_query)
        + mix_back(grad_keys, full_key)
        + mix_back(grad_values, full_value)
    )
    grad_picked_norm, grad_gain_a = norm_back(
        grad_normed, routed_tokens, inverse_attn, full_gain_attn
    )
    grad_picked = grad_picked_norm + grad_middle
    grad_router_w = jnp.sum(grad_logit[..., None] * routed_tokens, axis=(0, 1))
    grad_logit_full = place_rows(indicator_matrix, grad_logit[..., None])
    base = cotangent.astype(jnp.float32) + grad_logit_full * complete_router_weight.astype(
        jnp.float32
    )
    grad_hidden = (base + place_rows(indicator_matrix, grad_picked)).astype(jnp.bfloat16)
    shares = (
        lax.psum_scatter(
            grad_query_w.astype(jnp.bfloat16), "fsdp", scatter_dimension=0, tiled=True
        ).astype(jnp.float32),
        lax.psum_scatter(
            grad_key_w.astype(jnp.bfloat16), "fsdp", scatter_dimension=0, tiled=True
        ).astype(jnp.float32),
        lax.psum_scatter(
            grad_value_w.astype(jnp.bfloat16), "fsdp", scatter_dimension=0, tiled=True
        ).astype(jnp.float32),
        lax.psum_scatter(
            grad_out_w.astype(jnp.bfloat16), "fsdp", scatter_dimension=0, tiled=True
        ).astype(jnp.float32),
        lax.psum_scatter(
            up_weight_gradient.astype(jnp.bfloat16), "fsdp", scatter_dimension=0, tiled=True
        ).astype(jnp.float32),
        lax.psum_scatter(
            grad_down_w.astype(jnp.bfloat16), "fsdp", scatter_dimension=0, tiled=True
        ).astype(jnp.float32),
        lax.psum_scatter(
            grad_router_w.astype(jnp.bfloat16), "fsdp", scatter_dimension=0, tiled=True
        ).astype(jnp.float32),
        lax.psum_scatter(
            grad_gain_a.astype(jnp.bfloat16), "fsdp", scatter_dimension=0, tiled=True
        ).astype(jnp.float32),
        lax.psum_scatter(
            grad_gain_m.astype(jnp.bfloat16), "fsdp", scatter_dimension=0, tiled=True
        ).astype(jnp.float32),
    )
    summed = lax.psum(
        (
            shares[0],
            shares[1],
            shares[2],
            shares[3],
            shares[4],
            shares[5],
            shares[6],
            shares[7],
            shares[8],
        ),
        "rep",
    )
    return (
        out_hidden,
        grad_hidden,
        summed[0],
        summed[1],
        summed[2],
        summed[3],
        summed[4],
        summed[5],
        summed[6],
        summed[7],
        summed[8],
    )


def solution(mesh):
    placed = (
        P(("rep", "fsdp"), None, None),
        P(("rep", "fsdp"), None),
        P(("rep", "fsdp"), None),
        P("fsdp", None),
        P("fsdp", None),
        P("fsdp", None),
        P("fsdp", None),
        P("fsdp", None),
        P("fsdp", None),
        P("fsdp"),
        P("fsdp"),
        P("fsdp"),
        P(("rep", "fsdp"), None, None),
    )
    return jax.shard_map(
        on_device,
        mesh=mesh,
        in_specs=placed,
        out_specs=(
            P(("rep", "fsdp"), None, None),
            P(("rep", "fsdp"), None, None),
            P("fsdp", None),
            P("fsdp", None),
            P("fsdp", None),
            P("fsdp", None),
            P("fsdp", None),
            P("fsdp", None),
            P("fsdp"),
            P("fsdp"),
            P("fsdp"),
        ),
        check_vma=False,
    )
```

profile of v0, /device:TPU:0, one launch (start us, length us, event | category | flops | bytes accessed | tf_op | source)
XLA Modules:
  0.0 802.5 jit_solution(15990448095705318879)
XLA Ops:
  13.2 14.1 %all-reduce.8 = (bf16[768]{0:T(1024)(128)(2,1)S(1)}, bf16[768]{0:T(1024)(128)(2,1)S(1)}, bf16[768]{0:T(1024)(128)(2,1)S(1)}) all-reduce(bf16[768]{0:T(1024)(128)(2,1)S(1)} %dynamic-update-slice.1, bf16[768]{0:T(1024)(128)(2,1)S(1)} %dynamic-update-slice.2, bf16[768]{0:T(1024)(128)(2,1)S(1)} %dynamic-update-slice), channel_id=1, replica_groups=mesh['rep'=8,'fsdp'=4] {'fsdp'}, use_global_device_ids=true, to_apply=%add.1 | all-reduce | flops 2304 | bytes 9216
  28.0 6.7 gather_fusion.1
  34.7 6.6 multiply_reduce_fusion.8
  41.3 6.2 fusion.129
  47.5 6.7 gather_fusion
  57.1 3.4 convolution_convert_fusion.1
  62.0 12.3 %all-gather.9.cloned.1.call-done = bf16[768,768]{1,0:T(8,128)(2,1)} async-done(((bf16[192,768]{1,0:T(8,128)(2,1)}), bf16[768,768]{1,0:T(8,128)(2,1)}) %all-gather.9.cloned.1.call-update) | async-done | bytes 1179664 | tf_op jit(solution)/shard_map/all_gather | solution.py:75
  74.3 3.7 convolution_convert_fusion.2
  78.0 2.4 copy.131
  80.4 25.0 %all-gather.7.cloned.1.call-done = bf16[768,768]{1,0:T(8,128)(2,1)} async-done(((bf16[192,768]{1,0:T(8,128)(2,1)}), bf16[768,768]{1,0:T(8,128)(2,1)}) %all-gather.7.cloned.1.call-update) | async-done | bytes 1179664 | tf_op jit(solution)/shard_map/all_gather | solution.py:77
  105.5 3.7 convolution_convert_fusion.3
  109.2 2.5 copy.130
  111.7 3.1 fusion.18
  114.8 2.2 fusion.12
  118.5 3.8 fusion.85
  122.4 14.1 %all-gather.13.cloned.1.call-done = bf16[768,768]{1,0:T(8,128)(2,1)} async-done(((bf16[192,768]{1,0:T(8,128)(2,1)}), bf16[768,768]{1,0:T(8,128)(2,1)}) %all-gather.13.cloned.1.call-update) | async-done | bytes 1179664 | tf_op jit(solution)/shard_map/all_gather | solution.py:78
  136.5 5.0 multiply_reduce_fusion.7
  142.1 84.4 %all-gather.15.cloned.1.call-done = bf16[768,3072]{1,0:T(8,128)(2,1)} async-done(((bf16[192,3072]{1,0:T(8,128)(2,1)}), bf16[768,3072]{1,0:T(8,128)(2,1)}) %all-gather.15.cloned.1.call-update) | async-done | bytes 4718608 | tf_op jit(solution)/shard_map/all_gather | solution.py:79
  226.5 9.4 %fusion.76 = (u8[256,3072]{1,0:T(8,128)(4,1)S(1)}, u8[256,3072]{1,0:T(8,128)(4,1)S(1)}, f32[3,256,3072]{2,1,0:T(8,128)S(1)}) fusion(bf16[768,3072]{1,0:T(8,128)(2,1)} %all-gather.15.cloned.1.call-done, f32[3,256,768]{2,1,0:T(8,128)} %get-tuple-element.41, f32[768]{0:T(1024)S(1)} %convert_element_type.220, f32[3,256]{1,0:T(4,128)} %add_rsqrt_fusion), kind=kOutput, calls=%fused_computation.115 | convolution fusion | flops 3654746112 | bytes 18094080 | tf_op jit(solution)/shard_map/ska,ab->skb/dot_general | solution.py:27
  235.9 3.7 copy-done.5
  239.6 22.7 %multiply_convert_fusion = (bf16[3,256,3072]{2,1,0:T(8,128)(2,1)}, f32[3,256,3072]{2,1,0:T(8,128)}) fusion(f32[3,256,3072]{2,1,0:T(8,128)S(1)} %get-tuple-element.57, u8[256,3072]{1,0:T(8,128)(4,1)S(1)} %get-tuple-element.12, u8[256,3072]{1,0:T(8,128)(4,1)S(1)} %get-tuple-element.11), kind=kLoop, calls=%fused_computation.25 | loop fusion | flops 165150720 | bytes 25165824 | tf_op jit(solution)/shard_map/convert_element_type | solution.py:130
  262.3 53.5 %all-gather.17.cloned.1.call-done = bf16[3072,768]{1,0:T(8,128)(2,1)} async-done(((bf16[768,768]{1,0:T(8,128)(2,1)}), bf16[3072,768]{1,0:T(8,128)(2,1)}) %all-gather.17.cloned.1.call-update) | async-done | bytes 4718608 | tf_op jit(solution)/shard_map/all_gather | solution.py:80
  315.8 8.2 %fusion.82 = f32[3,256,768]{2,1,0:T(8,128)S(1)} fusion(f32[3,256,768]{2,1,0:T(8,128)} %get-tuple-element.56, bf16[3,256,3072]{2,1,0:T(8,128)(2,1)} %get-tuple-element.38, bf16[3072,768]{1,0:T(8,128)(2,1)} %all-gather.17.cloned.1.call-done), kind=kOutput, calls=%fused_computation.119 | convolution fusion | flops 3624468480 | bytes 14155776 | tf_op jit(solution)/shard_map/ska,ab->skb/dot_general | solution.py:27
  324.0 6.6 multiply_reduce_fusion.6
  331.4 12.5 %add_convert_fusion = bf16[3,256,3072]{2,1,0:T(8,128)(2,1)} fusion(f32[3,256,3072]{2,1,0:T(8,128)} %get-tuple-element.39, f32[3,256,3072]{2,1,0:T(8,128)} %copy-done.5, bf16[3072,768]{1,0:T(8,128)(2,1)} %all-gather.17.cloned.1.call-done, f32[3,256,768]{2,1,0:T(8,128)S(1)} %get-tuple-element.59, f32[3,256]{1,0:T(4,128)S(1)} %get-tuple-element.35), kind=kOutput, calls=%fused_computation.23 | convolution fusion | flops 3658088448 | bytes 30673920 | tf_op jit(solution)/shard_map/skb,ab->ska/dot_general | solution.py:31
  343.9 8.1 %multiply_reduce_fusion.1 = (bf16[768]{0:T(1024)(128)(2,1)}, f32[3,256]{1,0:T(4,128)S(1)}, f32[3,256,768]{2,1,0:T(8,128)S(1)}) fusion(f32[3,256,768]{2,1,0:T(8,128)S(1)} %copy-done.3, f32[3,256]{1,0:T(4,128)S(1)} %copy-done.28, f32[768]{0:T(1024)S(1)} %copy-done.26, bf16[3,256,3072]{2,1,0:T(8,128)(2,1)} %add_convert_fusion, ...), kind=kOutput, calls=%fused_computation.94 | convolution fusion | flops 3627416064 | bytes 14166528 | tf_op jit(solution)/shard_map/skb,ab->ska/dot_general | solution.py:31
  352.0 2.5 multiply_convert_fusion.6
  355.6 2.1 bitcast_convert_fusion.2
  359.4 3.8 convolution_convert_fusion
  363.2 2.4 copy.140
  365.6 6.3 fusion.86
  372.9 2.2 bitcast_convert_fusion.3
  375.1 6.8 fusion.130
  381.9 19.2 %multiply_convert_fusion.1 = bf16[3,12,64,256]{3,2,1,0:T(8,128)(2,1)} fusion(bf16[3,256,12,64]{1,3,2,0:T(8,128)(2,1)} %bitcast.122, f32[3,12,256,256]{2,3,1,0:T(8,128)} %fusion.130, f32[3,12,256,256]{2,3,1,0:T(8,128)} %copy-done.2, f32[3,12,256]{2,1,0:T(8,128)} %log_add_fusion, pred[3,256,256]{1,2,0:T(8,128)(4,1)} %compare_and_fusion), kind=kOutput, calls=%fused_computation.102 | convolution fusion | flops 329131264 | bytes 21467136 | tf_op jit(solution)/shard_map/shqk,sqhe->skhe/dot_general | solution.py:193
  401.1 3.8 bitcast_convert_fusion.4
  405.2 18.5 %multiply_convert_fusion.2 = bf16[3,12,64,256]{3,2,1,0:T(8,128)(2,1)} fusion(bf16[3,256,12,64]{1,3,2,0:T(8,128)(2,1)S(1)} %bitcast.120, f32[3,12,256,256]{2,3,1,0:T(8,128)} %fusion.130, f32[3,12,256,256]{2,3,1,0:T(8,128)} %copy-done.2, f32[3,12,256]{2,1,0:T(8,128)} %log_add_fusion, pred[3,256,256]{1,2,0:T(8,128)(4,1)} %compare_and_fusion), kind=kOutput, calls=%fused_computation.103 | convolution fusion | flops 329131264 | bytes 21467136 | tf_op jit(solution)/shard_map/shqk,skhe->sqhe/dot_general | solution.py:189
  423.7 3.8 bitcast_convert_fusion.5
  427.6 9.2 %bitcast_convert_fusion = bf16[3072,768]{1,0:T(8,128)(2,1)} fusion(bf16[3,256,3072]{2,1,0:T(8,128)(2,1)} %get-tuple-element.38, f32[3,256,768]{2,1,0:T(8,128)} %copy-done.12, f32[3,256]{1,0:T(4,128)S(1)} %copy-done.35), kind=kOutput, calls=%fused_computation.18 | convolution fusion | flops 3627417600 | bytes 11799552 | tf_op jit(solution)/shard_map/ska,skb->ab/dot_general | solution.py:35
  440.7 2.8 fusion.96
  445.2 2.7 multiply_reduce_fusion.2
  451.1 5.9 bitcast_convert_fusion.1
  457.7 10.0 %all-reduce.7 = (bf16[768]{0:T(1024)(128)(2,1)S(1)}, bf16[768]{0:T(1024)(128)(2,1)S(1)}, bf16[768]{0:T(1024)(128)(2,1)S(1)}) all-reduce(bf16[768]{0:T(1024)(128)(2,1)S(1)} %copy-done.37, bf16[768]{0:T(1024)(128)(2,1)S(1)} %copy-done.36, bf16[768]{0:T(1024)(128)(2,1)S(1)} %copy-done.41), channel_id=8, replica_groups=mesh['rep'=8,'fsdp'=4] {'fsdp'}, use_global_device_ids=true, to_apply=%region_21.22.clone | all-reduce | flops 2304 | bytes 9216
  467.8 23.0 %fusion.13 = f32[3,2048,2304]{2,1,0:T(8,128)} fusion(bf16[3,256,768]{2,1,0:T(8,128)(2,1)} %get-tuple-element.46, bf16[3,256,768]{2,1,0:T(8,128)(2,1)} %get-tuple-element.45, bf16[3,256,768]{2,1,0:T(8,128)(2,1)S(1)} %get-tuple-element.36, s32[3,256]{1,0:T(4,128)S(1)} %copy-done.16), kind=kOutput, calls=%fused_computation.43 | convolution fusion | flops 7259947008 | bytes 60165120 | tf_op jit(solution)/shard_map/ezy,ezf->eyf/dot_general | solution.py:45
  490.9 20.5 %fusion.16 = f32[3,2048,2304]{2,1,0:T(8,128)} fusion(bf16[3,256,768]{2,1,0:T(8,128)(2,1)S(1)} %copy-done.10, bf16[3,256,768]{2,1,0:T(8,128)(2,1)S(1)} %copy-done.11, bf16[3,256,768]{2,1,0:T(8,128)(2,1)S(1)} %copy-done.9, s32[3,256]{1,0:T(4,128)S(1)} %copy-done.16), kind=kOutput, calls=%fused_computation.46 | convolution fusion | flops 7259947008 | bytes 60165120 | tf_op jit(solution)/shard_map/ezy,ezf->eyf/dot_general | solution.py:45
  511.4 48.0 %fusion.2 = (bf16[3,2048,768]{2,1,0:T(8,128)(2,1)}, bf16[3,2048,768]{2,1,0:T(8,128)(2,1)}) fusion(f32[3,2048,2304]{2,1,0:T(8,128)} %fusion.13, bf16[3,2048,768]{2,1,0:T(8,128)(2,1)} %param.25, f32[768]{0:T(1024)S(1)} %copy-done.32, f32[3,2048]{1,0:T(4,128)S(1)} %bitcast.131, f32[3,2048,2304]{2,1,0:T(8,128)} %fusion.16, bf16[3,2048,768]{2,1,0:T(8,128)(2,1)} %param.13), kind=kLoop, calls=%fused_computation.5 | loop fusion | flops 56623104 | bytes 151022592 | tf_op jit(solution)/shard_map/convert_element_type | solution.py:217
  559.5 3.4 reduce-scatter.17.cloned.1.call-done
  562.9 88.0 %reduce-scatter.15.cloned.1.call-done = bf16[192,3072]{1,0:T(8,128)(2,1)} async-done(((bf16[768,3072]{1,0:T(8,128)(2,1)}), bf16[192,3072]{1,0:T(8,128)(2,1)}) %reduce-scatter.15.cloned.1.call-update) | async-done | bytes 1179664 | tf_op jit(solution)/shard_map/reduce_scatter | solution.py:231
  650.9 144.6 %all-reduce.10 = (f32[192,768]{1,0:T(8,128)}, f32[192,768]{1,0:T(8,128)}, f32[192,768]{1,0:T(8,128)}, f32[192,768]{1,0:T(8,128)}, f32[192,3072]{1,0:T(8,128)}, /...) all-reduce(bf16[192,768]{1,0:T(8,128)(2,1)} %reduce-scatter.7.clone, ...), channel_id=1, replica_groups=mesh['rep'=8,'fsdp'=4] {'rep'}, use_global_device_ids=true, to_apply=%region_9.10 | all-reduce | flops 1770048 | bytes 10621440 | tf_op jit(solution)/shard_map/psum | solution.py:247
  (167 shorter events, 26.1 us)
Async XLA Ops:
  7.2 20.8 %copy-start = (s32[3,2048]{1,0:T(4,128)S(1)}, s32[3,2048]{1,0:T(4,128)}, u32[]{:S(2)}) copy-start(s32[3,2048]{1,0:T(4,128)} %param.14) | copy-start | bytes 73732
  7.2 4.1 copy-start.42
  7.2 5.3 copy-start.44
  7.2 5.6 copy-start.45
  7.2 5.8 copy-start.46
  7.2 20.7 %copy-start.16 = (s32[3,256]{1,0:T(4,128)S(1)}, s32[3,256]{1,0:T(4,128)}, u32[]{:S(2)}) copy-start(s32[3,256]{1,0:T(4,128)} %param.15) | copy-start | bytes 9220
  7.2 48.8 %all-gather.11.cloned.1.call-start = ((), (), s32[]{:S(2)}) async-start(), calls=%async_computation.8 | async-start | bytes 1474560 | tf_op jit(solution)/shard_map/all_gather | solution.py:76
  8.0 66.3 %all-gather.9.cloned.1.call-start = ((), (), s32[]{:S(2)}) async-start(), calls=%async_computation.7 | async-start | bytes 1474560 | tf_op jit(solution)/shard_map/all_gather | solution.py:75
  8.7 96.7 %all-gather.7.cloned.1.call-start = ((), (), s32[]{:S(2)}) async-start(), calls=%async_computation.6 | async-start | bytes 1474560 | tf_op jit(solution)/shard_map/all_gather | solution.py:77
  9.5 127.0 %all-gather.13.cloned.1.call-start = ((), (), s32[]{:S(2)}) async-start(), calls=%async_computation.9 | async-start | bytes 1474560 | tf_op jit(solution)/shard_map/all_gather | solution.py:78
  10.0 216.4 %all-gather.15.cloned.1.call-start = ((), (), s32[]{:S(2)}) async-start(), calls=%async_computation.10 | async-start | bytes 5898240 | tf_op jit(solution)/shard_map/all_gather | solution.py:79
  10.6 305.2 %all-gather.17.cloned.1.call-start = ((), (), s32[]{:S(2)}) async-start(), calls=%async_computation.11 | async-start | bytes 5898240 | tf_op jit(solution)/shard_map/all_gather | solution.py:80
  11.2 548.2 %reduce-scatter.13.cloned.1.call-start = ((), (), s32[]{:S(2)}) async-start(), calls=%async_computation.15 | async-start | bytes 1474560 | tf_op jit(solution)/shard_map/reduce_scatter | solution.py:228
  27.9 198.5 %copy-start.25 = (f32[768]{0:T(1024)}, f32[768]{0:T(1024)S(1)}, u32[]{:S(2)}) copy-start(f32[768]{0:T(1024)S(1)} %convert_element_type.220) | copy-start | bytes 9220
  111.7 3.1 copy-start.13
  114.8 3.7 copy-start.2
  114.8 3.7 copy-start.22
  114.8 3.7 copy-start.8
  235.8 3.7 copy-start.5
  324.0 6.7 copy-start.33
  330.7 21.3 %copy-start.12 = (f32[3,256,768]{2,1,0:T(8,128)}, f32[3,256,768]{2,1,0:T(8,128)S(1)}, u32[]{:S(2)}) copy-start(f32[3,256,768]{2,1,0:T(8,128)S(1)} %get-tuple-element.59) | copy-start | bytes 7077892
  331.4 20.6 %copy-start.34 = (f32[3,256]{1,0:T(4,128)}, f32[3,256]{1,0:T(4,128)S(1)}, u32[]{:S(2)}) copy-start(f32[3,256]{1,0:T(4,128)S(1)} %get-tuple-element.35) | copy-start | bytes 9220
  331.4 12.5 %copy-start.3 = (f32[3,256,768]{2,1,0:T(8,128)S(1)}, f32[3,256,768]{2,1,0:T(8,128)}, u32[]{:S(2)}) copy-start(f32[3,256,768]{2,1,0:T(8,128)} %get-tuple-element.41) | copy-start | bytes 7077892
  331.4 12.5 %copy-start.26 = (f32[768]{0:T(1024)S(1)}, f32[768]{0:T(1024)}, u32[]{:S(2)}) copy-start(f32[768]{0:T(1024)} %copy-done.25) | copy-start | bytes 9220
  331.4 12.5 %copy-start.28 = (f32[3,256]{1,0:T(4,128)S(1)}, f32[3,256]{1,0:T(4,128)}, u32[]{:S(2)}) copy-start(f32[3,256]{1,0:T(4,128)} %add_rsqrt_fusion) | copy-start | bytes 9220
  352.0 3.6 copy-start.20
  357.7 201.7 %reduce-scatter.11.cloned.1.call-start = ((), (), s32[]{:S(2)}) async-start(), calls=%async_computation.14 | async-start | bytes 1474560 | tf_op jit(solution)/shard_map/reduce_scatter | solution.py:225
  365.6 7.3 copy-start.19
  375.1 184.4 %reduce-scatter.9.cloned.1.call-start = ((), (), s32[]{:S(2)}) async-start(), calls=%async_computation.13 | async-start | bytes 1474560 | tf_op jit(solution)/shard_map/reduce_scatter | solution.py:222
  405.0 154.5 %reduce-scatter.7.cloned.1.call-start = ((), (), s32[]{:S(2)}) async-start(), calls=%async_computation.12 | async-start | bytes 1474560 | tf_op jit(solution)/shard_map/reduce_scatter | solution.py:219
  423.7 3.9 copy-start.35
  427.6 135.4 %reduce-scatter.17.cloned.1.call-start = ((), (), s32[]{:S(2)}) async-start(), calls=%async_computation.17 | async-start | bytes 5898240 | tf_op jit(solution)/shard_map/reduce_scatter | solution.py:234
  436.8 214.1 %reduce-scatter.15.cloned.1.call-start = ((), (), s32[]{:S(2)}) async-start(), calls=%async_computation.16 | async-start | bytes 5898240 | tf_op jit(solution)/shard_map/reduce_scatter | solution.py:231
  438.8 4.7 copy-start.43
  438.8 4.7 copy-start.47
  445.1 2.7 copy-start.4
  445.2 2.7 copy-start.7
  445.2 2.7 copy-start.27
  445.2 2.7 copy-start.29
  445.2 2.7 copy-start.31
  445.2 5.9 slice-start
  447.9 3.2 slice-start.1
  467.8 23.0 %copy-start.9 = (bf16[3,256,768]{2,1,0:T(8,128)(2,1)S(1)}, bf16[3,256,768]{2,1,0:T(8,128)(2,1)}, u32[]{:S(2)}) copy-start(bf16[3,256,768]{2,1,0:T(8,128)(2,1)} %get-tuple-element.42) | copy-start | bytes 3538948
  467.8 23.0 %copy-start.10 = (bf16[3,256,768]{2,1,0:T(8,128)(2,1)S(1)}, bf16[3,256,768]{2,1,0:T(8,128)(2,1)}, u32[]{:S(2)}) copy-start(bf16[3,256,768]{2,1,0:T(8,128)(2,1)} %get-tuple-element.43) | copy-start | bytes 3538948
  467.8 23.0 %copy-start.11 = (bf16[3,256,768]{2,1,0:T(8,128)(2,1)S(1)}, bf16[3,256,768]{2,1,0:T(8,128)(2,1)}, u32[]{:S(2)}) copy-start(bf16[3,256,768]{2,1,0:T(8,128)(2,1)} %get-tuple-element.44) | copy-start | bytes 3538948
  490.8 20.5 %copy-start.24 = (f32[3,2048,1]{1,0,2:T(4,128)S(1)}, f32[3,2048,1]{1,0,2:T(4,128)}, u32[]{:S(2)}) copy-start(f32[3,2048,1]{1,0,2:T(4,128)} %copy.178) | copy-start | bytes 73732
  490.8 20.5 %copy-start.32 = (f32[768]{0:T(1024)S(1)}, f32[768]{0:T(1024)}, u32[]{:S(2)}) copy-start(f32[768]{0:T(1024)} %convert_element_type.238) | copy-start | bytes 9220
  511.4 284.1 %copy-start.1 = (s32[3,2048]{1,0:T(4,128)S(1)}, s32[3,2048]{1,0:T(4,128)}, u32[]{:S(2)}) copy-start(s32[3,2048]{1,0:T(4,128)} %param.14) | copy-start | bytes 73732
  (14 other events, 17.9 us)
Sparse Core Ops, SparseCore 0:
  9.7 32.8 all-gather.10
  44.1 30.1 all-gather.8
  75.9 29.5 all-gather.6
  106.9 29.5 all-gather.12
  137.9 88.5 all-gather.14
  227.9 87.8 all-gather.16
  357.8 27.6 reduce-scatter.12
  387.8 27.8 reduce-scatter.10
  418.1 27.8 reduce-scatter.8
  448.2 28.4 reduce-scatter.6
  478.9 83.9 reduce-scatter.16
  565.1 85.7 reduce-scatter.14
where the time goes:
time: 811 us; the launch traced here: 803 us
  waiting for transfers between devices  285 us (35%)
  matrix products  213 us (26%)
  blocking collectives  169 us (21%)
  other arithmetic  83.4 us (10%)
  local copies, waits for them, and re-layouts  35.2 us (4%)
  between operations  16.3 us (2%)
    psum x1, blocking collectives, on_device(): lax.psum((shares[0], shares[1], shares[2], shares[3], shares[4], shares[5...  145 us
    reduce_scatter x1, waiting for transfers between devices, on_device(): lax.psum_scatter(up_weight_gradient.astype(jnp.bfloat16), 'fsdp', scatter...  88 us
    all_gather x1, waiting for transfers between devices, on_device(): lax.all_gather(w_up, 'fsdp', axis=0, tiled=True)  84.4 us
    all_gather x1, waiting for transfers between devices, on_device(): lax.all_gather(w_down, 'fsdp', axis=0, tiled=True)  53.5 us
    convert_element_type x1, other arithmetic, on_device(): (base + place_rows(indicator_matrix, grad_picked)).astype(jnp.bfloat16)  48 us
    dot_general x3, matrix products, place_rows(): jnp.einsum('ezy,ezf->eyf', indicator, stacked, preferred_element_type=jnp...  44.7 us
    dot_general x6, matrix products, mix_rows(): jnp.einsum('ska,ab->skb', left, right, preferred_element_type=jnp.float32)  33.4 us
    dot_general x6, matrix products, mix_back(): jnp.einsum('skb,ab->ska', left, right, preferred_element_type=jnp.float32)  30.9 us
  transfers between devices with their start and end apart: 12, of which 7 were waited for; matrix products, arithmetic and copies ran while one was open for 35% of the time, Pallas kernels for 0%

commit v1 on v0

v1 whole, which is shorter than its diff:
```python
import functools

import jax
import jax.numpy as jnp
from jax import lax
from jax.experimental import pallas as pl
from jax.experimental.pallas import tpu as pltpu
from jax.sharding import PartitionSpec as P

HEADS = 12
HEAD_DIM = 64
PAIR = 2 * HEAD_DIM
EPSILON = 1e-06
F32 = jnp.float32
BF16 = jnp.bfloat16
TILE = 256
VECTOR_ROWS = 16
VMEM_BYTES = 56 * 1024 * 1024


def dot(left, right):
    return jnp.dot(left, right, preferred_element_type=F32)


def dot_nt(left, right):
    return lax.dot_general(left, right, (((1,), (1,)), ((), ())), preferred_element_type=F32)


def dot_tn(left, right):
    return lax.dot_general(left, right, (((0,), (0,)), ((), ())), preferred_element_type=F32)


def swap_bits(place):
    return ((place & 1) << 1) | (place >> 1)


def cost(flops, moved, transcendentals=0):
    return pl.CostEstimate(flops=flops, bytes_accessed=moved, transcendentals=transcendentals)


def params():
    return pltpu.CompilerParams(vmem_limit_bytes=VMEM_BYTES, dimension_semantics=None)


def column_of(row):
    size = row.shape[1]
    shape = (size, size)
    diagonal = lax.broadcasted_iota(jnp.int32, shape, 0) == lax.broadcasted_iota(jnp.int32, shape, 1)
    return jnp.sum(jnp.where(diagonal, row, 0.0), axis=1, keepdims=True)


def pick_kernel(with_mask, sel_ref, seg_ref, rows_ref, picked_ref, *rest):
    seq = pl.program_id(0)
    row = sel_ref[pl.ds(seq, 1), :].astype(F32)
    column = column_of(row)
    keep = row.shape[1]
    length = rows_ref.shape[1]
    places = lax.broadcasted_iota(jnp.int32, (keep, length), 1)
    chosen = jnp.where(column.astype(jnp.int32) == places, 1.0, 0.0).astype(BF16)
    picked_ref[0] = dot(chosen, rows_ref[0]).astype(BF16)
    if with_mask:
        (bias_ref,) = rest
        documents = jnp.broadcast_to(seg_ref[pl.ds(seq, 1), :].astype(F32), (8, length)).astype(BF16)
        of_column = dot_nt(chosen, documents)[:, :1]
        of_row = dot_nt(documents, chosen)[:1, :]
        allowed = (column >= row) & (of_column == of_row)
        bias_ref[0] = jnp.where(allowed, 0.0, -1e30).astype(BF16)


def pick_rows(selected, segments, rows, with_mask):
    seqs, length, width = rows.shape
    keep = selected.shape[1]
    whole = lambda a: pl.BlockSpec(a.shape, lambda s: (0, 0))
    out_shape = [jax.ShapeDtypeStruct((seqs, keep, width), BF16)]
    out_specs = [pl.BlockSpec((1, keep, width), lambda s: (s, 0, 0))]
    if with_mask:
        out_shape.append(jax.ShapeDtypeStruct((seqs, keep, keep), BF16))
        out_specs.append(pl.BlockSpec((1, keep, keep), lambda s: (s, 0, 0)))
    return pl.pallas_call(
        functools.partial(pick_kernel, with_mask),
        grid=(seqs,),
        in_specs=[whole(selected), whole(segments), pl.BlockSpec((1, length, width), lambda s: (s, 0, 0))],
        out_specs=out_specs,
        out_shape=out_shape,
        compiler_params=params(),
        cost_estimate=cost(2 * seqs * keep * length * width, rows.size * 2),
        name="pick_rows",
    )(selected, segments, rows)


def place_kernel(sel_ref, new_ref, base_ref, out_ref):
    seq, block = pl.program_id(0), pl.program_id(1)
    row = sel_ref[pl.ds(seq, 1), :]
    count = base_ref.shape[1]
    places = lax.broadcasted_iota(jnp.int32, (count, row.shape[1]), 0) + block * count
    hits = jnp.where(places == row, 1.0, 0.0)
    placed = dot(hits.astype(BF16), new_ref[0])
    hit = jnp.max(hits, axis=1, keepdims=True) > 0.0
    out_ref[0] = jnp.where(hit, placed, base_ref[0].astype(F32)).astype(BF16)


def place_rows(selected, new_rows, base):
    seqs, length, width = base.shape
    keep = selected.shape[1]
    count = length // 2
    return pl.pallas_call(
        place_kernel,
        grid=(seqs, length // count),
        in_specs=[
            pl.BlockSpec(selected.shape, lambda s, b: (0, 0)),
            pl.BlockSpec((1, keep, width), lambda s, b: (s, 0, 0)),
            pl.BlockSpec((1, count, width), lambda s, b: (s, b, 0)),
        ],
        out_specs=pl.BlockSpec((1, count, width), lambda s, b: (s, b, 0)),
        out_shape=jax.ShapeDtypeStruct(base.shape, BF16),
        compiler_params=params(),
        cost_estimate=cost(2 * seqs * keep * length * width, base.size * 4),
        name="place_rows",
    )(selected, new_rows.reshape(seqs, keep, width), base)


class Weight:
    def __init__(self, start, rows, columns, lanes):
        self.start, self.rows, self.columns, self.lanes = start, rows, columns, lanes


def weight_copies(idx_ref, parts, piece_refs, weight, own_ref, dst_ref, sem):
    shard, chip, core = idx_ref[0], idx_ref[1], idx_ref[2]
    shard_rows = own_ref.shape[0]
    lanes = weight.lanes
    own_at = pl.multiple_of(shard * shard_rows, 16)
    pltpu.make_async_copy(own_ref, dst_ref.at[pl.ds(own_at, shard_rows), :], sem).start()
    for (low, high, order), refs in zip(parts, piece_refs):
        for column in range(weight.columns):
            begin = weight.start + column * weight.rows
            lo, hi = max(begin, low), min(begin + weight.rows, high)
            if lo >= hi:
                continue
            for half in range(2):
                for second in range(2):
                    src = refs[2 * half + second]
                    for first in range(2):
                        x_bit, y_bit = (first, second) if order == "xy" else (second, first)
                        for other in range(3):
                            row = (shard ^ (other + 1)) * shard_rows + (chip ^ (2 * y_bit + x_bit)) * weight.rows
                            at = pl.multiple_of(row + (lo - begin), 16)
                            lane = pl.multiple_of((core ^ half) * (lanes * weight.columns) + column * lanes, 128)
                            pltpu.make_async_copy(
                                src.at[first, other, pl.ds(lo - low, hi - lo), :],
                                dst_ref.at[pl.ds(at, hi - lo), pl.ds(lane, lanes)],
                                sem,
                            ).start()

    def wait():
        pltpu.make_async_copy(dst_ref, dst_ref, sem).wait()

    return wait


def write_blocks(idx_ref, grad_ref, keep_ref, send_ref, start, rows, shard_rows):
    shard, chip, core = idx_ref[0], idx_ref[1], idx_ref[2]
    lanes = keep_ref.shape[-1]
    for x_bit in range(2):
        for y_bit in range(2):
            for place in range(4):
                row = (shard ^ swap_bits(place)) * shard_rows + (chip ^ (2 * y_bit + x_bit)) * rows
                at = pl.ds(pl.multiple_of(row, 16), rows)
                for half, out in ((0, keep_ref), (1, send_ref)):
                    lane = pl.ds(pl.multiple_of((core ^ half) * lanes, 128), lanes)
                    out[x_bit, y_bit, place, pl.ds(start, rows), :] = grad_ref[at, lane].astype(BF16)


def tiles_of(size):
    return size // TILE


def tile(index):
    return pl.ds(pl.multiple_of(index * TILE, TILE), TILE)


def loop(count, body):
    lax.fori_loop(0, count, lambda i, c: (body(i), c)[1], 0)


def inverse_rms(values):
    return lax.rsqrt(jnp.mean(values * values, axis=-1, keepdims=True) + EPSILON)


def attend_kernel(parts, weights, idx_ref, *refs):
    picked_ref, bias_ref, vec_ref, wq, wk, wv = refs[:6]
    count = 4 * len(parts)
    piece_refs = [refs[6 + 4 * i : 10 + 4 * i] for i in range(len(parts))]
    normed_ref, q_ref, k_ref, v_ref, probs_ref, att_ref, w_ref, sems = refs[6 + count :]
    seq = pl.program_id(0)
    keep = bias_ref.shape[1]
    seqs = picked_ref.shape[0] // keep

    @pl.when(seq == 0)
    def _():
        waits = [
            weight_copies(idx_ref, parts, piece_refs, weights[i], own, w_ref.at[i], sems.at[i])
            for i, own in enumerate((wq, wk, wv))
        ]
        gain = vec_ref[1:2, :]

        def norm(i):
            at = tile(i)
            values = picked_ref[at, :].astype(F32)
            normed_ref[at, :] = (values * inverse_rms(values) * gain).astype(BF16)

        loop(tiles_of(picked_ref.shape[0]), norm)
        for i, (out, scale) in enumerate(((q_ref, 0.125), (k_ref, 1.0), (v_ref, 1.0))):
            waits[i]()

            def project(n, i=i, out=out, scale=scale):
                result = dot(normed_ref[...], w_ref[i, :, tile(n)]).astype(BF16)
                out[:, tile(n)] = result * scale if scale != 1.0 else result

            loop(tiles_of(out.shape[1]), project)

    rows = pl.ds(pl.multiple_of(seq * keep, keep), keep)
    bias = bias_ref[0].astype(F32)
    low_half = lax.broadcasted_iota(jnp.int32, (keep, PAIR), 1) < HEAD_DIM

    def heads(pair):
        lanes = pl.ds(pl.multiple_of(pair * PAIR, PAIR), PAIR)
        queries, keys, values = q_ref[rows, lanes], k_ref[rows, lanes], v_ref[rows, lanes]
        results = []
        for half in range(2):
            mine = low_half if half == 0 else ~low_half
            scores = dot_nt(jnp.where(mine, queries, 0), keys) + bias
            exponent = jnp.exp(scores - jnp.max(scores, axis=-1, keepdims=True))
            probs = (exponent * (1.0 / jnp.sum(exponent, axis=-1, keepdims=True))).astype(BF16)
            probs_ref[0, 2 * pair + half] = probs
            results.append(dot(probs, values))
        att_ref[rows, lanes] = jnp.where(low_half, results[0], results[1]).astype(BF16)

    loop(HEADS // 2, heads)


def attend(idx, parts, weights, picked, bias, vectors, owns, pieces):
    tokens, width = picked.shape
    seqs, keep, _ = bias.shape
    fixed = lambda shape: pl.BlockSpec(shape, lambda s, i: (0,) * len(shape))
    anywhere = pl.BlockSpec(memory_space=pl.ANY)
    flat = jax.ShapeDtypeStruct((tokens, width), BF16)
    return pl.pallas_call(
        functools.partial(attend_kernel, parts, weights),
        grid_spec=pltpu.PrefetchScalarGridSpec(
            num_scalar_prefetch=1,
            grid=(seqs,),
            in_specs=[
                fixed((tokens, width)),
                pl.BlockSpec((1, keep, keep), lambda s, i: (s, 0, 0)),
                fixed(vectors.shape),
            ]
            + [anywhere] * (3 + len(pieces)),
            out_specs=[fixed((tokens, width))] * 4
            + [
                pl.BlockSpec((1, HEADS, keep, keep), lambda s, i: (s, 0, 0, 0)),
                fixed((tokens, width)),
            ],
            scratch_shapes=[pltpu.VMEM((3, width, width), BF16), pltpu.SemaphoreType.DMA((3,))],
        ),
        out_shape=[flat] * 4 + [jax.ShapeDtypeStruct((seqs, HEADS, keep, keep), BF16), flat],
        compiler_params=params(),
        cost_estimate=cost(2 * tokens * width * (3 * width + 8 * keep), tokens * width * 16),
        name="project_attend",
    )(idx, picked, bias, vectors, *owns, *pieces)


def gelu_parts(values):
    size = jnp.abs(values) * 0.7071067811865476
    bell = jnp.exp(-(size * size))
    t = 1.0 / (1.0 + 0.3275911 * size)
    poly = t * (0.254829592 + t * (-0.284496736 + t * (1.421413741 + t * (-1.453152027 + t * 1.061405429))))
    tail = 0.5 * poly * bell
    cdf = jnp.where(values >= 0.0, 1.0 - tail, tail)
    return values * cdf, cdf + values * (bell * 0.3989422804014327)


def up_kernel(parts, weights, idx_ref, *refs):
    att_ref, picked_ref, gbr_ref, vec_ref, w_out, w_up = refs[:6]
    count = 4 * len(parts)
    piece_refs = [refs[6 + 4 * i : 10 + 4 * i] for i in range(len(parts))]
    outs = refs[6 + count :]
    attn_ref, nm_ref, gmlp_ref, gating_ref, act_ref, slope_ref, keep_ref, send_ref, wo_ref, wu_ref, grad_ref, sems = outs
    step = pl.program_id(0)
    tokens = att_ref.shape[0]
    block = act_ref.shape[1]

    @pl.when(step == 0)
    def _():
        wait_out = weight_copies(idx_ref, parts, piece_refs, weights[0], w_out, wo_ref, sems.at[0])
        wait_up = weight_copies(idx_ref, parts, piece_refs, weights[1], w_up, wu_ref, sems.at[1])
        wait_out()

        def project(n):
            attn_ref[:, tile(n)] = dot(att_ref[...], wo_ref[:, tile(n)])

        loop(tiles_of(attn_ref.shape[1]), project)

        def norm(i):
            at = tile(i)
            values = picked_ref[at, :].astype(F32)
            middle = values + attn_ref[at, :]
            nm_ref[at, :] = (middle * inverse_rms(middle) * vec_ref[2:3, :]).astype(BF16)
            logit = jnp.sum(values * vec_ref[0:1, :], axis=-1, keepdims=True)
            gating = 1.0 / (1.0 + jnp.exp(-logit))
            gating_ref[at, :] = gating
            gmlp_ref[at, :] = (gating * gbr_ref[at, :].astype(F32)).astype(BF16)

        loop(tiles_of(tokens), norm)
        wait_up()

    base = (idx_ref[0] ^ swap_bits(step)) * block

    def columns(n):
        at = pl.ds(pl.multiple_of(base + n * TILE, TILE), TILE)
        before = dot(nm_ref[...], wu_ref[:, at])
        activated, slope = gelu_parts(before)
        activated = activated.astype(BF16)
        act_ref[:, tile(n)] = activated
        slope_ref[:, tile(n)] = slope.astype(BF16)
        grad_ref[tile(n), :] = dot_tn(activated, gmlp_ref[...])

    loop(tiles_of(block), columns)
    chip, core = idx_ref[1], idx_ref[2]
    rows, lanes = keep_ref.shape[-2:]
    for x_bit in range(2):
        for y_bit in range(2):
            at = pl.ds(pl.multiple_of((chip ^ (2 * y_bit + x_bit)) * rows, 16), rows)
            for half, out in ((0, keep_ref), (1, send_ref)):
                lane = pl.ds(pl.multiple_of((core ^ half) * lanes, 128), lanes)
                out[x_bit, y_bit, 0] = grad_ref[at, lane].astype(BF16)


def up(idx, parts, weights, attended, picked, branch_grad, vectors, owns, pieces):
    tokens, width = picked.shape
    hidden_units = owns[1].shape[1]
    block = hidden_units // 4
    rows, lanes = block // 4, width // 2
    fixed = lambda shape: pl.BlockSpec(shape, lambda s, i: (0,) * len(shape))
    anywhere = pl.BlockSpec(memory_space=pl.ANY)
    wide = pl.BlockSpec((tokens, block), lambda s, i: (0, i[0] ^ swap_bits(s)))
    grads = pl.BlockSpec((2, 2, 1, rows, lanes), lambda s, i: (0, 0, s, 0, 0))
    shape = jax.ShapeDtypeStruct
    return pl.pallas_call(
        functools.partial(up_kernel, parts, weights),
        grid_spec=pltpu.PrefetchScalarGridSpec(
            num_scalar_prefetch=1,
            grid=(4,),
            in_specs=[fixed((tokens, width))] * 3 + [fixed(vectors.shape)] + [anywhere] * (2 + len(pieces)),
            out_specs=[fixed((tokens, width))] * 3 + [fixed((tokens, 1)), wide, wide, grads, grads],
            scratch_shapes=[
                pltpu.VMEM((width, width), BF16),
                pltpu.VMEM((width, hidden_units), BF16),
                pltpu.VMEM((block, width), F32),
                pltpu.SemaphoreType.DMA((2,)),
            ],
        ),
        out_shape=[
            shape((tokens, width), F32),
            shape((tokens, width), BF16),
            shape((tokens, width), BF16),
            shape((tokens, 1), F32),
            shape((tokens, hidden_units), BF16),
            shape((tokens, hidden_units), BF16),
            shape((2, 2, 4, rows, lanes), BF16),
            shape((2, 2, 4, rows, lanes), BF16),
        ],
        compiler_params=params(),
        cost_estimate=cost(2 * tokens * width * (width + 2 * hidden_units), tokens * hidden_units * 8),
        name="project_up",
    )(idx, attended, picked, branch_grad, vectors, *owns, *pieces)


def norm_back(grad_normed, values, inverse, gain):
    scaled = grad_normed * gain
    grad_gain = jnp.sum(grad_normed * values * inverse, axis=0, keepdims=True)
    grad_values = inverse * scaled - values * (inverse * inverse * inverse) * jnp.mean(
        scaled * values, axis=-1, keepdims=True
    )
    return grad_values, grad_gain


def down_kernel(parts_up, weight_up, parts_down, weight_down, idx_ref, *refs):
    act_ref, slope_ref, nm_ref, gmlp_ref, attn_ref, picked_ref, gbr_ref, gating_ref, vec_ref, w_up, w_down = refs[:11]
    at = 11
    pieces_up = [refs[at + 4 * i : at + 4 * i + 4] for i in range(len(parts_up))]
    at += 4 * len(parts_up)
    pieces_down = [refs[at + 4 * i : at + 4 * i + 4] for i in range(len(parts_down))]
    at += 4 * len(parts_down)
    new_ref, gattn_ref, gmid_ref, glogit_ref, ggain_ref, keep_ref, send_ref = refs[at : at + 7]
    wu_ref, wd_ref, nmt_ref, mlp_ref, gnm_ref, grad_ref, sems = refs[at + 7 :]
    step = pl.program_id(0)
    tokens, block = act_ref.shape
    core = idx_ref[2]

    @pl.when(step == 0)
    def _():
        wait_up = weight_copies(idx_ref, parts_up, pieces_up, weight_up, w_up, wu_ref, sems.at[0])
        wait_down = weight_copies(idx_ref, parts_down, pieces_down, weight_down, w_down, wd_ref, sems.at[1])

        def turn(n):
            nmt_ref[tile(n), :] = nm_ref[:, tile(n)].T

        loop(tiles_of(nm_ref.shape[1]), turn)
        mlp_ref[...] = jnp.zeros_like(mlp_ref)
        gnm_ref[...] = jnp.zeros_like(gnm_ref)
        wait_up()
        wait_down()

    base = (step ^ (2 * core)) * block

    def columns(n):
        at = pl.ds(pl.multiple_of(base + n * TILE, TILE), TILE)
        down = wd_ref[at, :]
        mlp_ref[...] += dot(act_ref[:, tile(n)], down)
        grad_act = dot_nt(gmlp_ref[...], down)
        grad_before = (grad_act * slope_ref[:, tile(n)].astype(F32)).astype(BF16)
        grad_ref[:, tile(n)] = dot(nmt_ref[...], grad_before)
        gnm_ref[...] += dot_nt(grad_before, wu_ref[:, at])

    loop(tiles_of(block), columns)
    shard, chip = idx_ref[0], idx_ref[1]
    rows = weight_up.rows
    lanes = keep_ref.shape[-1]
    shard_rows = w_up.shape[0]

    def write(out):
        for x_bit in range(2):
            for y_bit in range(2):
                for place in range(4):
                    row = (shard ^ swap_bits(place)) * shard_rows + (chip ^ (2 * y_bit + x_bit)) * rows
                    at = pl.ds(pl.multiple_of(row, 16), rows)
                    for part in range(block // lanes):
                        out[x_bit, y_bit, place, pl.ds(part * rows, rows), :] = grad_ref[
                            at, pl.ds(part * lanes, lanes)
                        ].astype(BF16)

    @pl.when(step < 2)
    def _():
        write(keep_ref)

    @pl.when(step >= 2)
    def _():
        write(send_ref)

    @pl.when(step == pl.num_programs(0) - 1)
    def _():
        ggain_ref[...] = jnp.zeros_like(ggain_ref)

        def finish(i):
            at = tile(i)
            attention = attn_ref[at, :]
            values = picked_ref[at, :].astype(F32)
            gating = gating_ref[at, :]
            branch_grad = gbr_ref[at, :].astype(F32)
            delta = attention + mlp_ref[at, :]
            new_ref[at, :] = (values + gating * delta).astype(BF16)
            grad_gating = jnp.sum(branch_grad * delta, axis=-1, keepdims=True)
            glogit_ref[at, :] = grad_gating * gating * (1.0 - gating)
            middle = values + attention
            grad_middle, grad_gain = norm_back(gnm_ref[at, :], middle, inverse_rms(middle), vec_ref[2:3, :])
            gmid_ref[at, :] = grad_middle
            gattn_ref[at, :] = (gating * branch_grad + grad_middle).astype(BF16)
            ggain_ref[0:1, :] += grad_gain

        loop(tiles_of(tokens), finish)


def down(idx, parts_up, weight_up, parts_down, weight_down, arrays, vectors, owns, pieces):
    activated, slope, normed, grad_mlp, attn_out, picked, branch_grad, gating = arrays
    tokens, width = picked.shape
    hidden_units = activated.shape[1]
    block = hidden_units // 4
    lanes = width // 2
    parts_of = block // lanes
    rows = weight_up.rows
    fixed = lambda shape: pl.BlockSpec(shape, lambda s, i: (0,) * len(shape))
    anywhere = pl.BlockSpec(memory_space=pl.ANY)
    wide = pl.BlockSpec((tokens, block), lambda s, i: (0, s ^ (2 * i[2])))
    grads = lambda at: pl.BlockSpec((2, 2, 4, parts_of * rows, lanes), lambda s, i: (0, 0, 0, at(s), 0))
    shape = jax.ShapeDtypeStruct
    flat = fixed((tokens, width))
    column = fixed((tokens, 1))
    grad_shape = shape((2, 2, 4, 2 * parts_of * rows, lanes), BF16)
    return pl.pallas_call(
        functools.partial(down_kernel, parts_up, weight_up, parts_down, weight_down),
        grid_spec=pltpu.PrefetchScalarGridSpec(
            num_scalar_prefetch=1,
            grid=(4,),
            in_specs=[wide, wide] + [flat] * 5 + [column, fixed(vectors.shape)] + [anywhere] * (2 + len(pieces)),
            out_specs=[flat] * 3
            + [
                column,
                fixed((8, width)),
                grads(lambda s: jnp.minimum(s, 1)),
                grads(lambda s: jnp.maximum(s, 2) - 2),
            ],
            scratch_shapes=[
                pltpu.VMEM((width, hidden_units), BF16),
                pltpu.VMEM((hidden_units, width), BF16),
                pltpu.VMEM((width, tokens), BF16),
                pltpu.VMEM((tokens, width), F32),
                pltpu.VMEM((tokens, width), F32),
                pltpu.VMEM((width, block), F32),
                pltpu.SemaphoreType.DMA((2,)),
            ],
        ),
        out_shape=[
            shape((tokens, width), BF16),
            shape((tokens, width), BF16),
            shape((tokens, width), F32),
            shape((tokens, 1), F32),
            shape((8, width), F32),
            grad_shape,
            grad_shape,
        ],
        compiler_params=params(),
        cost_estimate=cost(2 * tokens * width * 4 * hidden_units, tokens * hidden_units * 8),
        name="project_down_and_back",
    )(idx, activated, slope, normed, grad_mlp, attn_out, picked, branch_grad, gating, vectors, *owns, *pieces)


def attend_back_kernel(parts, weight, idx_ref, *refs):
    gattn_ref, att_ref, q_ref, k_ref, v_ref, probs_ref, w_out = refs[:7]
    count = 4 * len(parts)
    piece_refs = [refs[7 + 4 * i : 11 + 4 * i] for i in range(len(parts))]
    gq_ref, gk_ref, gv_ref, keep_ref, send_ref, w_ref, gatt_ref, grad_ref, sems = refs[7 + count :]
    seq = pl.program_id(0)
    keep = probs_ref.shape[2]

    @pl.when(seq == 0)
    def _():
        wait = weight_copies(idx_ref, parts, piece_refs, weight, w_out, w_ref, sems.at[0])

        def grads(n):
            grad_ref[tile(n), :] = dot_tn(att_ref[:, tile(n)], gattn_ref[...])

        loop(tiles_of(att_ref.shape[1]), grads)
        write_blocks(idx_ref, grad_ref, keep_ref, send_ref, 0, weight.rows, w_out.shape[0])
        wait()

        def project(n):
            gatt_ref[:, tile(n)] = dot_nt(gattn_ref[...], w_ref[tile(n), :]).astype(BF16)

        loop(tiles_of(att_ref.shape[1]), project)

    rows = pl.ds(pl.multiple_of(seq * keep, keep), keep)
    low_half = lax.broadcasted_iota(jnp.int32, (keep, PAIR), 1) < HEAD_DIM

    def heads(pair):
        lanes = pl.ds(pl.multiple_of(pair * PAIR, PAIR), PAIR)
        queries, keys, values = q_ref[rows, lanes], k_ref[rows, lanes], v_ref[rows, lanes]
        grad_att = gatt_ref[rows, lanes]
        found = []
        for half in range(2):
            mine = low_half if half == 0 else ~low_half
            probs = probs_ref[0, 2 * pair + half]
            grad_values = dot_tn(probs, grad_att)
            wide = probs.astype(F32)
            weighted = wide * dot_nt(jnp.where(mine, grad_att, 0), values)
            scores = (weighted - wide * jnp.sum(weighted, axis=-1, keepdims=True)).astype(BF16)
            found.append((dot(scores, keys) * 0.125, dot_tn(scores, queries), grad_values))
        for out, first, second in zip((gq_ref, gk_ref, gv_ref), *found):
            out[rows, lanes] = jnp.where(low_half, first, second).astype(BF16)

    loop(HEADS // 2, heads)


def attend_back(idx, parts, weight, grad_attn, attended, queries, keys, values, probs, own, pieces):
    tokens, width = grad_attn.shape
    seqs, _, keep, _ = probs.shape
    lanes = width // 2
    fixed = lambda shape: pl.BlockSpec(shape, lambda s, i: (0,) * len(shape))
    anywhere = pl.BlockSpec(memory_space=pl.ANY)
    flat = fixed((tokens, width))
    grad_shape = (2, 2, 4, weight.rows, lanes)
    shape = jax.ShapeDtypeStruct
    return pl.pallas_call(
        functools.partial(attend_back_kernel, parts, weight),
        grid_spec=pltpu.PrefetchScalarGridSpec(
            num_scalar_prefetch=1,
            grid=(seqs,),
            in_specs=[flat] * 5
            + [pl.BlockSpec((1, HEADS, keep, keep), lambda s, i: (s, 0, 0, 0))]
            + [anywhere] * (1 + len(pieces)),
            out_specs=[flat] * 3 + [fixed(grad_shape)] * 2,
            scratch_shapes=[
                pltpu.VMEM((width, width), BF16),
                pltpu.VMEM((tokens, width), BF16),
                pltpu.VMEM((width, width), F32),
                pltpu.SemaphoreType.DMA((1,)),
            ],
        ),
        out_shape=[shape((tokens, width), BF16)] * 3 + [shape(grad_shape, BF16)] * 2,
        compiler_params=params(),
        cost_estimate=cost(2 * tokens * width * (2 * width + 20 * keep), tokens * width * 24),
        name="attend_back",
    )(idx, grad_attn, attended, queries, keys, values, probs, own, *pieces)


def project_back_kernel(parts, weights, idx_ref, *refs):
    gq_ref, gk_ref, gv_ref, normed_ref, picked_ref, gmid_ref, gbr_ref, glogit_ref, vec_ref, ggain_ref = refs[:10]
    wq, wk, wv = refs[10:13]
    count = 4 * len(parts)
    piece_refs = [refs[13 + 4 * i : 17 + 4 * i] for i in range(len(parts))]
    new_ref, keep_ref, send_ref, w_ref, nt_ref, gn_ref, grad_ref, sum_ref, sems = refs[13 + count :]
    waits = [
        weight_copies(idx_ref, parts, piece_refs, weights[i], own, w_ref.at[i], sems.at[i])
        for i, own in enumerate((wq, wk, wv))
    ]
    width = normed_ref.shape[1]

    def turn(n):
        nt_ref[tile(n), :] = normed_ref[:, tile(n)].T

    loop(tiles_of(width), turn)
    for i, grad in enumerate((gq_ref, gk_ref, gv_ref)):
        def grads(n, grad=grad):
            grad_ref[:, tile(n)] = dot(nt_ref[...], grad[:, tile(n)])

        loop(tiles_of(width), grads)
        write_blocks(idx_ref, grad_ref, keep_ref, send_ref, i * weights[i].rows, weights[i].rows, wq.shape[0])
        waits[i]()

        def project(n, i=i, grad=grad):
            result = dot_nt(grad[...], w_ref[i, tile(n), :])
            gn_ref[:, tile(n)] = result if i == 0 else gn_ref[:, tile(n)] + result

        loop(tiles_of(width), project)
    sum_ref[...] = jnp.zeros_like(sum_ref)

    def finish(i):
        at = tile(i)
        values = picked_ref[at, :].astype(F32)
        grad_picked, grad_gain = norm_back(gn_ref[at, :], values, inverse_rms(values), vec_ref[1:2, :])
        grad_logit = glogit_ref[at, :]
        new_ref[at, :] = (
            gbr_ref[at, :].astype(F32) + grad_logit * vec_ref[0:1, :] + (grad_picked + gmid_ref[at, :])
        ).astype(BF16)
        sum_ref[0:1, :] += jnp.sum(grad_logit * values, axis=0, keepdims=True)
        sum_ref[1:2, :] += grad_gain

    loop(tiles_of(picked_ref.shape[0]), finish)
    sum_ref[2:3, :] = ggain_ref[0:1, :]
    lanes = keep_ref.shape[-1]
    start = sum(weight.rows for weight in weights)
    lows = sum_ref[:, :lanes]
    highs = sum_ref[:, lanes:]
    both = jnp.concatenate([lows, highs], axis=0).astype(BF16)
    for x_bit in range(2):
        for y_bit in range(2):
            for place in range(4):
                for out in (keep_ref, send_ref):
                    out[x_bit, y_bit, place, pl.ds(start, VECTOR_ROWS), :] = both


def project_back(idx, parts, weights, arrays, vectors, grad_gain, owns, pieces):
    tokens, width = arrays[0].shape
    lanes = width // 2
    fixed = lambda shape: pl.BlockSpec(shape, lambda g, i: (0,) * len(shape))
    anywhere = pl.BlockSpec(memory_space=pl.ANY)
    flat = fixed((tokens, width))
    grad_shape = (2, 2, 4, sum(weight.rows for weight in weights) + VECTOR_ROWS, lanes)
    shape = jax.ShapeDtypeStruct
    return pl.pallas_call(
        functools.partial(project_back_kernel, parts, weights),
        grid_spec=pltpu.PrefetchScalarGridSpec(
            num_scalar_prefetch=1,
            grid=(1,),
            in_specs=[flat] * 7
            + [fixed((tokens, 1)), fixed(vectors.shape), fixed(grad_gain.shape)]
            + [anywhere] * (3 + len(pieces)),
            out_specs=[flat] + [fixed(grad_shape)] * 2,
            scratch_shapes=[
                pltpu.VMEM((3, width, width), BF16),
                pltpu.VMEM((width, tokens), BF16),
                pltpu.VMEM((tokens, width), F32),
                pltpu.VMEM((width, width), F32),
                pltpu.VMEM((8, width), F32),
                pltpu.SemaphoreType.DMA((3,)),
            ],
        ),
        out_shape=[shape((tokens, width), BF16)] + [shape(grad_shape, BF16)] * 2,
        compiler_params=params(),
        cost_estimate=cost(2 * tokens * width * 6 * width, tokens * width * 30),
        name="project_back",
    )(idx, *arrays, vectors, grad_gain, *owns, *pieces)


def solution(mesh):
    replicas, shards = mesh.shape["rep"], mesh.shape["fsdp"]
    rep_pairs = lambda bit: [(i, i ^ bit) for i in range(replicas)]
    shard_pairs = lambda bit: [(i, i ^ bit) for i in range(shards)]
    groups = [list(range(i, i + 8)) for i in range(0, replicas, 8)]
    plane = {"c": 1, "x": 2, "y": 4}

    def swap(values, way):
        return lax.ppermute(values, "rep", rep_pairs(plane[way]))

    def swap_shard(values, bit):
        return lax.ppermute(values, "fsdp", shard_pairs(bit))

    def gather_shards(own):
        second = swap_shard(own, 2)
        pair = swap_shard(jnp.stack([own, second]), 1)
        return jnp.stack([pair[0], second, pair[1]])

    def gather_plane(blocks, parts):
        pieces = []
        for low, high, order in parts:
            mine = blocks[:, low:high]
            both = jnp.stack([mine, swap(mine, order[0])])
            other = swap(both, order[1])
            pieces += [both, other, swap(both, "c"), swap(other, "c")]
        return pieces

    def add(left, right):
        return (left.astype(F32) + right.astype(F32)).astype(BF16)

    def reduce_blocks(keep, send, order):
        got = swap(send, "c")
        if order == "yx":
            keep, got = keep.swapaxes(0, 1), got.swapaxes(0, 1)
        for way in order:
            away, keep = add(keep[1], got[1]), add(keep[0], got[0])
            got = swap(away, way)
        keep, got = [a.reshape((2, 2) + a.shape[1:]) for a in (keep, got)]
        for bit in (1, 2):
            away, keep = add(keep[1], got[1]), add(keep[0], got[0])
            got = swap_shard(away, bit)
        total = keep.astype(F32) + got.astype(F32)
        bit = 8
        while bit < replicas:
            total = total + lax.ppermute(total, "rep", rep_pairs(bit))
            bit *= 2
        return total

    def gather_rows(total):
        return lax.all_gather(
            total.astype(BF16), "rep", axis=0, tiled=False, axis_index_groups=groups if len(groups) > 1 else None
        )

    def unpack(rows, weight, start):
        part = rows[:, start : start + weight.rows * weight.columns]
        part = part.reshape(4, 2, weight.columns, weight.rows, weight.lanes)
        part = part.transpose(0, 3, 1, 2, 4)
        return part.reshape(4 * weight.rows, 2 * weight.columns * weight.lanes).astype(F32)

    def on_device(
        hidden,
        segments,
        selected,
        w_query,
        w_key,
        w_value,
        w_out,
        w_up,
        w_down,
        w_router,
        gain_attn,
        gain_mlp,
        cotangent,
    ):
        seqs, length, width = hidden.shape
        keep = selected.shape[1]
        tokens = seqs * keep
        lanes = width // 2
        place = lax.axis_index("rep") % 8
        shard, chip, core = lax.axis_index("fsdp"), place // 2, place % 2
        idx = jnp.stack([shard, chip, core]).astype(jnp.int32)

        def cut(weight):
            rows, columns = weight.shape[0] // 4, weight.shape[1] // 2
            block = lax.dynamic_slice(weight, (chip * rows, core * columns), (rows, columns))
            parts = columns // lanes
            if parts > 1:
                block = block.reshape(rows, parts, lanes).swapaxes(0, 1).reshape(rows * parts, lanes)
            return block

        small, tall = w_query.shape[0] // 4, w_down.shape[0] // 4
        wide = w_up.shape[1] // 2 // lanes
        q_at, k_at, v_at = [Weight(i * small, small, 1, lanes) for i in range(3)]
        out_at, up_at = Weight(0, small, 1, lanes), Weight(small, small, wide, lanes)
        down_at = Weight(0, tall, 1, lanes)
        first_rows = 3 * small
        first_parts = [(0, 64, "xy"), (64, first_rows, "yx")]
        second_rows = small + small * wide
        second_parts = [(0, 128, "xy"), (128, second_rows, "yx")]
        third_parts = [(0, tall // 2, "xy"), (tall // 2, tall, "yx")]

        with jax.named_scope("gather_weights"):
            vectors = jnp.stack([w_router, gain_attn, gain_mlp])
            first_own = jnp.concatenate([cut(w) for w in (w_query, w_key, w_value)])
            padded = jnp.pad(vectors, ((0, VECTOR_ROWS - 3), (0, lanes - vectors.shape[1])))
            first = gather_shards(jnp.concatenate([first_own, padded]))
            first_pieces = gather_plane(first, first_parts)
            second = gather_shards(jnp.concatenate([cut(w_out), cut(w_up)]))
            second_pieces = gather_plane(second, second_parts)
            third = gather_shards(cut(w_down))
            third_pieces = gather_plane(third, third_parts)
            others = first[:, first_rows : first_rows + 3, : vectors.shape[1]]
            by_place = jnp.concatenate([vectors[None], others])
            at = jnp.arange(shards)
            vec = sum(
                jnp.where((at == (shard ^ i))[None, :, None], by_place[i][:, None, :], 0) for i in range(shards)
            )
            vec = jnp.pad(vec.reshape(3, width).astype(F32), ((0, 5), (0, 0)))

        picked, bias = pick_rows(selected, segments, hidden, True)
        (branch_grad,) = pick_rows(selected, segments, cotangent, False)
        picked, branch_grad = picked.reshape(tokens, width), branch_grad.reshape(tokens, width)
        normed, queries, keys, values, probs, attended = attend(
            idx, first_parts, (q_at, k_at, v_at), picked, bias, vec, (w_query, w_key, w_value), first_pieces
        )
        attn_out, normed_mlp, grad_mlp, gating, activated, slope, down_keep, down_send = up(
            idx, second_parts, (out_at, up_at), attended, picked, branch_grad, vec, (w_out, w_up), second_pieces
        )
        with jax.named_scope("reduce_down"):
            total_down = gather_rows(reduce_blocks(down_keep, down_send, "xy"))
        new_rows, grad_attn, grad_middle, grad_logit, grad_gain_m, up_keep, up_send = down(
            idx,
            second_parts,
            up_at,
            third_parts,
            down_at,
            (activated, slope, normed_mlp, grad_mlp, attn_out, picked, branch_grad, gating),
            vec,
            (w_up, w_down),
            second_pieces + third_pieces,
        )
        with jax.named_scope("reduce_up"):
            total_up = gather_rows(reduce_blocks(up_keep, up_send, "yx"))
        grad_q, grad_k, grad_v, out_keep, out_send = attend_back(
            idx, second_parts, out_at, grad_attn, attended, queries, keys, values, probs, w_out, second_pieces
        )
        grad_rows, first_keep, first_send = project_back(
            idx,
            first_parts,
            (q_at, k_at, v_at),
            (grad_q, grad_k, grad_v, normed, picked, grad_middle, branch_grad, grad_logit),
            vec,
            grad_gain_m,
            (w_query, w_key, w_value),
            first_pieces,
        )
        with jax.named_scope("reduce_out"):
            total_out = gather_rows(reduce_blocks(out_keep, out_send, "xy"))
        with jax.named_scope("reduce_first"):
            summed = reduce_blocks(first_keep, first_send, "yx")
            total_first = gather_rows(summed[:first_rows])
            sums = summed[first_rows:].reshape(2, 8, lanes)[:, :3].swapaxes(0, 1).reshape(3, width)
            sums = lax.dynamic_slice(sums, (0, shard * w_router.shape[0]), (3, w_router.shape[0]))
        out_hidden = place_rows(selected, new_rows, hidden)
        grad_hidden = place_rows(selected, grad_rows, cotangent)
        return (
            out_hidden,
            grad_hidden,
            unpack(total_first, q_at, 0),
            unpack(total_first, k_at, small),
            unpack(total_first, v_at, 2 * small),
            unpack(total_out, out_at, 0),
            unpack(total_up, up_at, 0),
            unpack(total_down, down_at, 0),
            sums[0],
            sums[1],
            sums[2],
        )

    placed = (
        P(("rep", "fsdp"), None, None),
        P(("rep", "fsdp"), None),
        P(("rep", "fsdp"), None),
        P("fsdp", None),
        P("fsdp", None),
        P("fsdp", None),
        P("fsdp", None),
        P("fsdp", None),
        P("fsdp", None),
        P("fsdp"),
        P("fsdp"),
        P("fsdp"),
        P(("rep", "fsdp"), None, None),
    )
    return jax.shard_map(
        on_device,
        mesh=mesh,
        in_specs=placed,
        out_specs=(
            P(("rep", "fsdp"), None, None),
            P(("rep", "fsdp"), None, None),
            P("fsdp", None),
            P("fsdp", None),
            P("fsdp", None),
            P("fsdp", None),
            P("fsdp", None),
            P("fsdp", None),
            P("fsdp"),
            P("fsdp"),
            P("fsdp"),
        ),
        check_vma=False,
    )
```

time: 811 us -> 407 us (0.50)
  matrix products: 213 us -> 0 us
  waiting for transfers between devices: 285 us -> 96.6 us
  Pallas kernels: 0 us -> 177 us
  blocking collectives: 169 us -> 20.8 us
  other arithmetic: 83.4 us -> 23.4 us
  starting transfers between devices: 1.26 us -> 47.7 us
  local copies, waits for them, and re-layouts: 35.2 us -> 25 us
    dot_general x30 -> x0, matrix products: 213 us -> none  [the longest x3 44.7 us: place_rows(): jnp.einsum('ezy,ezf->eyf', indicator, stacked, preferred_element_type=jnp...]
    all_gather x6 -> x2, waiting for transfers between devices: 189 us -> 0.01 us  [gather_rows(): lax.all_gather(total.astype(BF16), 'rep', axis=0, tiled=False, axis_index...]
    pallas_call x0 -> x9, Pallas kernels: none -> 177 us  [the longest x1 36 us: down(): pl.pallas_call(functools.partial(down_kernel, parts_up, weight_up, parts_...]
    psum x1 -> x0, blocking collectives: 145 us -> none  [on_device(): lax.psum((shares[0], shares[1], shares[2], shares[3], shares[4], shares[5...]
    ppermute x0 -> x50, waiting for transfers between devices: none -> 96.5 us  [the longest x36 70.8 us: swap(): return lax.ppermute(values, 'rep', rep_pairs(plane[way]))]
    reduce_scatter x6 -> x0, waiting for transfers between devices: 91.5 us -> none  [the longest x1 88 us: on_device(): lax.psum_scatter(up_weight_gradient.astype(jnp.bfloat16), 'fsdp', scatter...]
    convert_element_type x13 -> x24, other arithmetic: 78.1 us -> 21.4 us  [the longest x18 16.2 us: add(): return (left.astype(F32) + right.astype(F32)).astype(BF16)]
    ppermute x0 -> x50, starting transfers between devices: none -> 47.6 us  [the longest x36 27.4 us: swap(): return lax.ppermute(values, 'rep', rep_pairs(plane[way]))]
  transfers between devices with their start and end apart: 12 -> 52, of which waited for: 7 -> 15; matrix products, arithmetic and copies ran while one was open for 35% -> 10% of each run, Pallas kernels for 0% -> 44%
where the time goes in v1:
time: 407 us; the launch traced here: 406 us
  Pallas kernels  177 us (43%)
  waiting for transfers between devices  96.6 us (24%)
  starting transfers between devices  47.7 us (12%)
  local copies, waits for them, and re-layouts  25 us (6%)
  other arithmetic  23.4 us (6%)
  blocking collectives  20.8 us (5%)
  between operations  14.9 us (4%)
    ppermute x36, waiting for transfers between devices, swap(): return lax.ppermute(values, 'rep', rep_pairs(plane[way]))  70.8 us
    pallas_call x1, Pallas kernels, down(): pl.pallas_call(functools.partial(down_kernel, parts_up, weight_up, parts_...  36 us
    pallas_call x1, Pallas kernels, up(): pl.pallas_call(functools.partial(up_kernel, parts, weights), grid_spec=pl...  33.5 us
    pallas_call x1, Pallas kernels, attend(): pl.pallas_call(functools.partial(attend_kernel, parts, weights), grid_spe...  27.4 us
    ppermute x36, starting transfers between devices, swap(): return lax.ppermute(values, 'rep', rep_pairs(plane[way]))  27.4 us
    pallas_call x1, Pallas kernels, attend_back(): pl.pallas_call(functools.partial(attend_back_kernel, parts, weight), grid...  25.9 us
    ppermute x14, waiting for transfers between devices, swap_shard(): return lax.ppermute(values, 'fsdp', shard_pairs(bit))  25.8 us
    pallas_call x2, Pallas kernels, place_rows(): pl.pallas_call(place_kernel, grid=(seqs, length // count), in_specs=[pl.B...  21.1 us
  transfers between devices with their start and end apart: 52, of which 15 were waited for; matrix products, arithmetic and copies ran while one was open for 10% of the time, Pallas kernels for 44%

profile of v1, /device:TPU:0, one launch (start us, length us, event | category | flops | bytes accessed | tf_op | source)
XLA Modules:
  0.0 405.7 jit_solution(12310024308980564545)
XLA Ops:
  9.1 4.1 %collective-permute-start.10 = (bf16[240,384]{1,0:T(8,128)(2,1)S(1)}, bf16[240,384]{1,0:T(8,128)(2,1)S(1)}, u32[]{:S(2)}, u32[]{:S(2)}) collective-permute-start(bf16[240,384]{1,0:T(8,128)(2,1)S(1)} %get-tuple-element.111), channel_id=1, source_target_pairs={{0,2},{1,3},{2,0},{3,1},{4,6},{5,7},{6,4},{7,5},{8,10},{9,11},{10,... | collective-permute-start | bytes 552968 | tf_op jit(solution)/shard_map/gather_weights/ppermute | solution.py:705
  18.6 3.0 collective-permute-start.20
  21.6 7.7 %pick_rows.2 = (bf16[3,256,768]{2,1,0:T(8,128)(2,1)}, bf16[3,256,256]{2,1,0:T(8,128)(2,1)}) custom-call(s32[3,256]{1,0:T(4,128)} %sel_ref.7, s32[3,2048]{1,0:T(4,128)} %seg_ref.3, bf16[3,2048,768]{2,1,0:T(8,128)(2,1)} %base_ref.2), custom_call_target="tpu_custom_call" | custom-call | flops 2415919104 | bytes 9437184 | tf_op jit(solution)/shard_map/pick_rows/pallas_call | solution.py:79
  29.3 6.8 %pick_rows.3 = bf16[3,256,768]{2,1,0:T(8,128)(2,1)} custom-call(s32[3,256]{1,0:T(4,128)} %sel_ref.7, s32[3,2048]{1,0:T(4,128)} %seg_ref.3, bf16[3,2048,768]{2,1,0:T(8,128)(2,1)} %base_ref.3), custom_call_target="tpu_custom_call" | custom-call | flops 2415919104 | bytes 9437184 | tf_op jit(solution)/shard_map/pick_rows/pallas_call | solution.py:79
  38.4 1.6 collective-permute-start.1
  40.8 1.6 collective-permute-start.11
  42.4 5.0 %collective-permute-done.1 = bf16[2,160,384]{2,1,0:T(8,128)(2,1)S(1)} collective-permute-done((bf16[2,160,384]{2,1,0:T(8,128)(2,1)S(1)}, bf16[2,160,384]{2,1,0:T(8,128)(2,1)S(1)}, u32[]{:S(2)}, u32[]{:S(2)}) %collective-permute-start.1) | collective-permute-done | bytes 245792 | tf_op jit(solution)/shard_map/gather_weights/ppermute | solution.py:705
  47.4 1.6 collective-permute-start.6
  50.6 3.1 collective-permute-done.21
  53.9 1.6 collective-permute-start.22
  57.6 2.0 collective-permute-done.11
  59.7 1.6 collective-permute-start.12
  61.3 1.6 collective-permute-start.16
  63.8 3.3 collective-permute-done.12
  67.2 3.2 collective-permute-done.16
  73.5 1.6 collective-permute-done.7.refs_11_.refs_18_
  76.3 17.2 %collective-permute-done.23.refs_20_ = bf16[2,3,96,384]{3,2,1,0:T(8,128)(2,1)} collective-permute-done((bf16[2,3,96,384]{3,2,1,0:T(8,128)(2,1)S(1)}, bf16[2,3,96,384]{3,2,1,0:T(8,128)(2,1)}, u32[]{:S(2)}, u32[]{:S(2)}) %collective-permute-start.23) | collective-permute-done | bytes 442400 | tf_op jit(solution)/shard_map/gather_weights/ppermute | solution.py:702
  94.6 2.5 collective-permute-start.27
  97.1 27.4 %project_attend.1 = (bf16[768,768]{1,0:T(8,128)(2,1)}, bf16[768,768]{1,0:T(8,128)(2,1)}, bf16[768,768]{1,0:T(8,128)(2,1)}, bf16[768,768]{1,0:T(8,128)(2,1)}, bf1...) custom-call(s32[3]{0:T(128)} %pad_add_fusion.idx_ref, bf16[768,768]{1,0:T(8,128)(2,1)} %bitcast.292, ...), custom_call_target="tpu_custom_call" | custom-call | flops 5133828096 | bytes 9437184 | tf_op jit(solution)/shard_map/project_attend/pallas_call | solution.py:247
  126.6 33.5 %project_up.1 = (f32[768,768]{1,0:T(8,128)}, bf16[768,768]{1,0:T(8,128)(2,1)}, bf16[768,768]{1,0:T(8,128)(2,1)}, f32[768,1]{1,0:T(8,128)}, bf16[768,3072]{1,0:T(...) custom-call(s32[3]{0:T(128)} %pad_add_fusion.idx_ref, ...), custom_call_target="tpu_custom_call" | custom-call | flops 8153726976 | bytes 18874368 | tf_op jit(solution)/shard_map/project_up/pallas_call | solution.py:348
  161.4 36.0 %project_down_and_back.1 = (bf16[768,768]{1,0:T(8,128)(2,1)}, bf16[768,768]{1,0:T(8,128)(2,1)}, f32[768,768]{1,0:T(8,128)}, f32[768,1]{1,0:T(8,128)}, f32[8,768]...) custom-call(s32[3]{0:T(128)} %pad_add_fusion.idx_ref, ...), custom_call_target="tpu_custom_call" | custom-call | flops 14495514624 | bytes 18874368 | tf_op jit(solution)/shard_map/project_down_and_back/pallas_call | solution.py:489
  197.9 25.9 %attend_back.1 = (bf16[768,768]{1,0:T(8,128)(2,1)}, bf16[768,768]{1,0:T(8,128)(2,1)}, bf16[768,768]{1,0:T(8,128)(2,1)}, bf16[2,2,4,48,384]{4,3,2,1,0:T(8,128)(2,1)}, bf16[2,2,4,48,384]{4,3,2,1,0:T(8,128)(2,1)}) custom-call(s32[3]{0:T(128)} %pad_add_fusion.idx_ref, bf16[768,768]{1,0:T(8,128)(2,1)} %get-tuple-element.52.refs_0_, ...), custom_call_target="tpu_custom_call" | custom-call | flops 7851737088 | bytes 14155776 | tf_op jit(solution)/shard_map/attend_back/pallas_call | solution.py:582
  223.7 1.7 add_convert_fusion.1
  226.2 18.8 %project_back.1 = (bf16[768,768]{1,0:T(8,128)(2,1)}, bf16[2,2,4,160,384]{4,3,2,1,0:T(8,128)(2,1)}, bf16[2,2,4,160,384]{4,3,2,1,0:T(8,128)(2,1)}) custom-call(s32[3]{0:T(128)} %pad_add_fusion.idx_ref, bf16[768,768]{1,0:T(8,128)(2,1)} %get-tuple-element.57.refs_0_, bf16[768,768]{1,0:T(8,128)(2,1)} %get-tuple-element.58.refs_1_, ...), custom_call_target="tpu_custom_call" | custom-call | flops 5435817984 | bytes 17694720 | tf_op jit(solution)/shard_map/project_back/pallas_call | solution.py:669
  245.5 2.1 copy.58
  248.0 10.6 %place_rows.3 = bf16[3,2048,768]{2,1,0:T(8,128)(2,1)} custom-call(s32[3,256]{1,0:T(4,128)} %sel_ref.7, bf16[3,256,768]{2,1,0:T(8,128)(2,1)} %bitcast.273, bf16[3,2048,768]{2,1,0:T(8,128)(2,1)} %base_ref.3), custom_call_target="tpu_custom_call" | custom-call | flops 2415919104 | bytes 18874368 | tf_op jit(solution)/shard_map/place_rows/pallas_call | solution.py:106
  262.7 1.8 collective-permute-start.47
  264.6 1.6 fusion.3
  266.5 2.4 collective-permute-done.36
  269.7 1.7 collective-permute-start.37
  271.4 2.4 fusion.8
  274.1 5.0 %collective-permute-done.47 = bf16[4,192,384]{2,1,0:T(8,128)(2,1)S(1)} collective-permute-done((bf16[4,192,384]{2,1,0:T(8,128)(2,1)S(1)}, bf16[4,192,384]{2,1,0:T(8,128)(2,1)S(1)}, u32[]{:S(2)}, u32[]{:S(2)}) %collective-permute-start.47) | collective-permute-done | bytes 589856 | tf_op jit(solution)/shard_map/reduce_down/ppermute | solution.py:702
  279.2 1.6 collective-permute-start.48
  280.8 1.6 add_convert_fusion.2
  282.4 4.2 %collective-permute-done.48 = bf16[2,192,384]{2,1,0:T(8,128)(2,1)S(1)} collective-permute-done((bf16[2,192,384]{2,1,0:T(8,128)(2,1)S(1)}, bf16[2,192,384]{2,1,0:T(8,128)(2,1)S(1)}, u32[]{:S(2)}, u32[]{:S(2)}) %collective-permute-start.48) | collective-permute-done | bytes 294944 | tf_op jit(solution)/shard_map/reduce_down/ppermute | solution.py:705
  286.7 17.6 %collective-permute-done.41 = bf16[2,4,192,384]{3,2,1,0:T(8,128)(2,1)S(1)} collective-permute-done((bf16[2,4,192,384]{3,2,1,0:T(8,128)(2,1)S(1)}, bf16[2,4,192,384]{3,2,1,0:T(8,128)(2,1)S(1)}, u32[]{:S(2)}, u32[]{:S(2)}) %collective-permute-start.41) | collective-permute-done | bytes 1179680 | tf_op jit(solution)/shard_map/reduce_up/ppermute | solution.py:702
  308.6 1.6 collective-permute-start.38
  311.7 19.9 %collective-permute-done.31 = bf16[2,4,160,384]{3,2,1,0:T(8,128)(2,1)S(1)} collective-permute-done((bf16[2,4,160,384]{3,2,1,0:T(8,128)(2,1)}, bf16[2,4,160,384]{3,2,1,0:T(8,128)(2,1)S(1)}, u32[]{:S(2)}, u32[]{:S(2)}) %collective-permute-start.31) | collective-permute-done | bytes 983072 | tf_op jit(solution)/shard_map/reduce_first/ppermute | solution.py:702
  333.6 1.7 collective-permute-start.43
  335.3 10.5 %place_rows.2 = bf16[3,2048,768]{2,1,0:T(8,128)(2,1)} custom-call(s32[3,256]{1,0:T(4,128)} %sel_ref.7, bf16[3,256,768]{2,1,0:T(8,128)(2,1)} %bitcast.272, bf16[3,2048,768]{2,1,0:T(8,128)(2,1)} %base_ref.2), custom_call_target="tpu_custom_call" | custom-call | flops 2415919104 | bytes 18874368 | tf_op jit(solution)/shard_map/place_rows/pallas_call | solution.py:106
  346.0 3.0 collective-permute-start.44
  349.5 4.8 %collective-permute-done.44 = bf16[192,384]{1,0:T(8,128)(2,1)S(1)} collective-permute-done((bf16[192,384]{1,0:T(8,128)(2,1)S(1)}, bf16[192,384]{1,0:T(8,128)(2,1)S(1)}, u32[]{:S(2)}, u32[]{:S(2)}) %collective-permute-start.44) | collective-permute-done | bytes 147488 | tf_op jit(solution)/shard_map/reduce_up/ppermute | solution.py:705
  356.0 10.3 %all-gather.1 = bf16[384,384]{1,0:T(8,128)(2,1)S(1)} all-gather(bf16[48,384]{1,0:T(8,128)(2,1)S(1)} %fusion.36), channel_id=3, replica_groups=mesh['rep'=8,'fsdp'=4] {'rep'}, dimensions={0}, use_global_device_ids=true | all-gather | bytes 331776 | tf_op jit(solution)/shard_map/reduce_out/all_gather | solution.py:743
  368.3 6.7 %collective-permute-done.34 = bf16[160,384]{1,0:T(8,128)(2,1)S(1)} collective-permute-done((bf16[160,384]{1,0:T(8,128)(2,1)S(1)}, bf16[160,384]{1,0:T(8,128)(2,1)S(1)}, u32[]{:S(2)}, u32[]{:S(2)}) %collective-permute-start.34) | collective-permute-done | bytes 122912 | tf_op jit(solution)/shard_map/reduce_first/ppermute | solution.py:705
  375.1 10.5 %all-gather = bf16[1152,384]{1,0:T(8,128)(2,1)S(1)} all-gather(bf16[144,384]{1,0:T(8,128)(2,1)S(1)} %slice.584), channel_id=2, replica_groups=mesh['rep'=8,'fsdp'=4] {'rep'}, dimensions={0}, use_global_device_ids=true | all-gather | bytes 995328 | tf_op jit(solution)/shard_map/reduce_first/all_gather | solution.py:743
  391.0 1.8 copy.48
  392.9 1.6 copy.55
  396.8 2.0 reshape.330
  (226 shorter events, 51.6 us)
Async XLA Ops:
  7.2 382.4 %all-gather.9.cloned.1.call-start = ((), (), s32[]{:S(2)}) async-start(), calls=%async_computation.1 | async-start | bytes 1327104 | tf_op jit(solution)/shard_map/reduce_down/all_gather | solution.py:743
  9.1 31.6 %collective-permute-start.10 = (bf16[240,384]{1,0:T(8,128)(2,1)S(1)}, bf16[240,384]{1,0:T(8,128)(2,1)S(1)}, u32[]{:S(2)}, u32[]{:S(2)}) collective-permute-start(bf16[240,384]{1,0:T(8,128)(2,1)S(1)} %get-tuple-element.111), channel_id=1, source_target_pairs={{0,2},{1,3},{2,0},{3,1},{4,6},{5,7},{6,4},{7,5},{8,10},{9,11},{10,... | collective-permute-start | bytes 552968 | tf_op jit(solution)/shard_map/gather_weights/ppermute | solution.py:705
  17.5 20.8 %collective-permute-start = (bf16[160,384]{1,0:T(8,128)(2,1)S(1)}, bf16[160,384]{1,0:T(8,128)(2,1)S(1)}, u32[]{:S(2)}, u32[]{:S(2)}) collective-permute-start(bf16[160,384]{1,0:T(8,128)(2,1)S(1)} %fusion.33), channel_id=1, source_target_pairs={{0,2},{1,3},{2,0},{3,1},{4,6},{5,7},{6,4},{7,5},{8,10},{9,11},{10,... | collective-permute-start | bytes 368648 | tf_op jit(solution)/shard_map/gather_weights/ppermute | solution.py:705
  18.6 21.6 %collective-permute-start.20 = (bf16[192,384]{1,0:T(8,128)(2,1)S(1)}, bf16[192,384]{1,0:T(8,128)(2,1)S(1)}, u32[]{:S(2)}, u32[]{:S(2)}) collective-permute-start(bf16[192,384]{1,0:T(8,128)(2,1)S(1)} %dynamic_slice.26), channel_id=1, source_target_pairs={{0,2},{1,3},{2,0},{3,1},{4,6},{5,7},{6,4},{7,5},{8,10},{9,11},{10,... | collective-permute-start | bytes 442376 | tf_op jit(solution)/shard_map/gather_weights/ppermute | solution.py:705
  38.4 9.0 %collective-permute-start.1 = (bf16[2,160,384]{2,1,0:T(8,128)(2,1)S(1)}, bf16[2,160,384]{2,1,0:T(8,128)(2,1)S(1)}, u32[]{:S(2)}, u32[]{:S(2)}) collective-permute-start(bf16[2,160,384]{2,1,0:T(8,128)(2,1)S(1)} %pad_maximum_fusion.11), channel_id=1, source_target_pairs={{0,1},{1,0},{2,3},{3,2},{4,5},{5,4},{6,7},{7,6},{8,9},{9,8},{10,11... | collective-permute-start | bytes 737288 | tf_op jit(solution)/shard_map/gather_weights/ppermute | solution.py:705
  40.2 13.5 %collective-permute-start.21 = (bf16[2,192,384]{2,1,0:T(8,128)(2,1)S(1)}, bf16[2,192,384]{2,1,0:T(8,128)(2,1)S(1)}, u32[]{:S(2)}, u32[]{:S(2)}) collective-permute-start(bf16[2,192,384]{2,1,0:T(8,128)(2,1)S(1)} %pad_maximum_fusion.9), channel_id=1, source_target_pairs={{0,1},{1,0},{2,3},{3,2},{4,5},{5,4},{6,7},{7,6},{8,9},{9,8},{10,11... | collective-permute-start | bytes 884744 | tf_op jit(solution)/shard_map/gather_weights/ppermute | solution.py:705
  40.8 18.8 %collective-permute-start.11 = (bf16[2,240,384]{2,1,0:T(8,128)(2,1)S(1)}, bf16[2,240,384]{2,1,0:T(8,128)(2,1)S(1)}, u32[]{:S(2)}, u32[]{:S(2)}) collective-permute-start(bf16[2,240,384]{2,1,0:T(8,128)(2,1)S(1)} %pad_maximum_fusion.7), channel_id=1, source_target_pairs={{0,1},{1,0},{2,3},{3,2},{4,5},{5,4},{6,7},{7,6},{8,9},{9,8},{10,11... | collective-permute-start | bytes 1105928 | tf_op jit(solution)/shard_map/gather_weights/ppermute | solution.py:705
  47.4 13.9 %collective-permute-start.6 = (bf16[3,80,384]{2,1,0:T(8,128)(2,1)S(1)}, bf16[3,80,384]{2,1,0:T(8,128)(2,1)S(1)}, u32[]{:S(2)}, u32[]{:S(2)}) collective-permute-start(bf16[3,80,384]{2,1,0:T(8,128)(2,1)S(1)} %pad_maximum_fusion.12), channel_id=1, source_target_pairs={{0,16},{4,20},{8,24},{12,28},{16,0},{20,4},{24,8},{28,12},{1,17},{... | collective-permute-start | bytes 552968 | tf_op jit(solution)/shard_map/gather_weights/ppermute | solution.py:702
  53.9 9.1 %collective-permute-start.22 = (bf16[3,96,384]{2,1,0:T(8,128)(2,1)S(1)}, bf16[3,96,384]{2,1,0:T(8,128)(2,1)S(1)}, u32[]{:S(2)}, u32[]{:S(2)}) collective-permute-start(bf16[3,96,384]{2,1,0:T(8,128)(2,1)S(1)} %get-tuple-element.99), channel_id=1, source_target_pairs={{0,8},{4,12},{8,0},{12,4},{16,24},{20,28},{24,16},{28,20},{1,9},{5... | collective-permute-start | bytes 663560 | tf_op jit(solution)/shard_map/gather_weights/ppermute | solution.py:702
  57.0 15.0 %collective-permute-start.3 = (bf16[2,3,64,384]{3,2,1,0:T(8,128)(2,1)S(1)}, bf16[2,3,64,384]{3,2,1,0:T(8,128)(2,1)S(1)}, u32[]{:S(2)}, u32[]{:S(2)}) collective-permute-start(bf16[2,3,64,384]{3,2,1,0:T(8,128)(2,1)S(1)} %pad_maximum_fusion.8.refs_6_.refs_13_), channel_id=1, source_target_pairs={{0,16},{4,20},{8,24},{12,28},{16,0},{20,4},{24,8},{28,12},{1,17},{... | collective-permute-start | bytes 884744 | tf_op jit(solution)/shard_map/gather_weights/ppermute | solution.py:702
  61.3 9.0 %collective-permute-start.16 = (bf16[3,112,384]{2,1,0:T(8,128)(2,1)S(1)}, bf16[3,112,384]{2,1,0:T(8,128)(2,1)S(1)}, u32[]{:S(2)}, u32[]{:S(2)}) collective-permute-start(bf16[3,112,384]{2,1,0:T(8,128)(2,1)S(1)} %pad_maximum_fusion.10), channel_id=1, source_target_pairs={{0,16},{4,20},{8,24},{12,28},{16,0},{20,4},{24,8},{28,12},{1,17},{... | collective-permute-start | bytes 774152 | tf_op jit(solution)/shard_map/gather_weights/ppermute | solution.py:702
  63.0 9.5 %collective-permute-start.4 = (bf16[2,3,64,384]{3,2,1,0:T(8,128)(2,1)S(1)}, bf16[2,3,64,384]{3,2,1,0:T(8,128)(2,1)S(1)}, u32[]{:S(2)}, u32[]{:S(2)}) collective-permute-start(bf16[2,3,64,384]{3,2,1,0:T(8,128)(2,1)S(1)} %pad_maximum_fusion.8.refs_6_.refs_13_), channel_id=1, source_target_pairs={{0,4},{4,0},{8,12},{12,8},{16,20},{20,16},{24,28},{28,24},{1,5},{5... | collective-permute-start | bytes 884744 | tf_op jit(solution)/shard_map/gather_weights/ppermute | solution.py:702
  63.2 11.9 %collective-permute-start.7 = (bf16[2,3,80,384]{3,2,1,0:T(8,128)(2,1)S(1)}, bf16[2,3,80,384]{3,2,1,0:T(8,128)(2,1)}, u32[]{:S(2)}, u32[]{:S(2)}) collective-permute-start(bf16[2,3,80,384]{3,2,1,0:T(8,128)(2,1)S(1)} %pad_maximum_fusion.6.refs_10_.refs_17_), channel_id=1, source_target_pairs={{0,8},{4,12},{8,0},{12,4},{16,24},{20,28},{24,16},{28,20},{1,9},{5... | collective-permute-start | bytes 1105928 | tf_op jit(solution)/shard_map/gather_weights/ppermute | solution.py:702
  67.1 8.0 %collective-permute-start.8 = (bf16[2,3,80,384]{3,2,1,0:T(8,128)(2,1)S(1)}, bf16[2,3,80,384]{3,2,1,0:T(8,128)(2,1)}, u32[]{:S(2)}, u32[]{:S(2)}) collective-permute-start(bf16[2,3,80,384]{3,2,1,0:T(8,128)(2,1)S(1)} %pad_maximum_fusion.6.refs_10_.refs_17_), channel_id=1, source_target_pairs={{0,4},{4,0},{8,12},{12,8},{16,20},{20,16},{24,28},{28,24},{1,5},{5... | collective-permute-start | bytes 1105928 | tf_op jit(solution)/shard_map/gather_weights/ppermute | solution.py:702
  70.4 23.7 %collective-permute-start.13 = (bf16[2,3,128,384]{3,2,1,0:T(8,128)(2,1)S(1)}, bf16[2,3,128,384]{3,2,1,0:T(8,128)(2,1)S(1)}, u32[]{:S(2)}, u32[]{:S(2)}) collective-permute-start(bf16[2,3,128,384]{3,2,1,0:T(8,128)(2,1)S(1)} %pad_maximum_fusion.refs_6_.refs_11_.refs_7_), channel_id=1, source_target_pairs={{0,16},{4,20},{8,24},{12,28},{16,0},{20,4},{24,8},{28,12},{1,17},{... | collective-permute-start | bytes 1769480 | tf_op jit(solution)/shard_map/gather_weights/ppermute | solution.py:702
  72.0 21.5 %collective-permute-start.23 = (bf16[2,3,96,384]{3,2,1,0:T(8,128)(2,1)S(1)}, bf16[2,3,96,384]{3,2,1,0:T(8,128)(2,1)}, u32[]{:S(2)}, u32[]{:S(2)}) collective-permute-start(bf16[2,3,96,384]{3,2,1,0:T(8,128)(2,1)S(1)} %pad_maximum_fusion.4.refs_19_), channel_id=1, source_target_pairs={{0,16},{4,20},{8,24},{12,28},{16,0},{20,4},{24,8},{28,12},{1,17},{... | collective-permute-start | bytes 1327112 | tf_op jit(solution)/shard_map/gather_weights/ppermute | solution.py:702
  72.6 21.4 %collective-permute-start.17 = (bf16[2,3,112,384]{3,2,1,0:T(8,128)(2,1)S(1)}, bf16[2,3,112,384]{3,2,1,0:T(8,128)(2,1)}, u32[]{:S(2)}, u32[]{:S(2)}) collective-permute-start(bf16[2,3,112,384]{3,2,1,0:T(8,128)(2,1)S(1)} %pad_maximum_fusion.2.refs_10_.refs_15_.refs_11_), channel_id=1, source_target_pairs={{0,8},{4,12},{8,0},{12,4},{16,24},{20,28},{24,16},{28,20},{1,9},{5... | collective-permute-start | bytes 1548296 | tf_op jit(solution)/shard_map/gather_weights/ppermute | solution.py:702
  75.1 18.3 %collective-permute-start.5 = (bf16[2,3,64,384]{3,2,1,0:T(8,128)(2,1)}, bf16[2,3,64,384]{3,2,1,0:T(8,128)(2,1)S(1)}, u32[]{:S(2)}, u32[]{:S(2)}) collective-permute-start(bf16[2,3,64,384]{3,2,1,0:T(8,128)(2,1)} %copy-done.22), channel_id=1, source_target_pairs={{0,4},{4,0},{8,12},{12,8},{16,20},{20,16},{24,28},{28,24},{1,5},{5... | collective-permute-start | bytes 884744 | tf_op jit(solution)/shard_map/gather_weights/ppermute | solution.py:702
  75.1 19.4 %collective-permute-start.9 = (bf16[2,3,80,384]{3,2,1,0:T(8,128)(2,1)}, bf16[2,3,80,384]{3,2,1,0:T(8,128)(2,1)S(1)}, u32[]{:S(2)}, u32[]{:S(2)}) collective-permute-start(bf16[2,3,80,384]{3,2,1,0:T(8,128)(2,1)} %collective-permute-done.7.refs_11_.refs_18_), channel_id=1, source_target_pairs={{0,4},{4,0},{8,12},{12,8},{16,20},{20,16},{24,28},{28,24},{1,5},{5... | collective-permute-start | bytes 1105928 | tf_op jit(solution)/shard_map/gather_weights/ppermute | solution.py:702
  93.5 31.2 %collective-permute-start.18 = (bf16[2,3,112,384]{3,2,1,0:T(8,128)(2,1)S(1)}, bf16[2,3,112,384]{3,2,1,0:T(8,128)(2,1)S(1)}, u32[]{:S(2)}, u32[]{:S(2)}) collective-permute-start(bf16[2,3,112,384]{3,2,1,0:T(8,128)(2,1)S(1)} %pad_maximum_fusion.2.refs_10_.refs_15_.refs_11_), channel_id=1, source_target_pairs={{0,4},{4,0},{8,12},{12,8},{16,20},{20,16},{24,28},{28,24},{1,5},{5... | collective-permute-start | bytes 1548296 | tf_op jit(solution)/shard_map/gather_weights/ppermute | solution.py:702
  93.5 31.8 %collective-permute-start.14 = (bf16[2,3,128,384]{3,2,1,0:T(8,128)(2,1)S(1)}, bf16[2,3,128,384]{3,2,1,0:T(8,128)(2,1)S(1)}, u32[]{:S(2)}, u32[]{:S(2)}) collective-permute-start(bf16[2,3,128,384]{3,2,1,0:T(8,128)(2,1)S(1)} %pad_maximum_fusion.refs_6_.refs_11_.refs_7_), channel_id=1, source_target_pairs={{0,4},{4,0},{8,12},{12,8},{16,20},{20,16},{24,28},{28,24},{1,5},{5... | collective-permute-start | bytes 1769480 | tf_op jit(solution)/shard_map/gather_weights/ppermute | solution.py:702
  94.0 31.4 %collective-permute-start.19 = (bf16[2,3,112,384]{3,2,1,0:T(8,128)(2,1)}, bf16[2,3,112,384]{3,2,1,0:T(8,128)(2,1)S(1)}, u32[]{:S(2)}, u32[]{:S(2)}) collective-permute-start(bf16[2,3,112,384]{3,2,1,0:T(8,128)(2,1)} %collective-permute-done.17.refs_11_.refs_16_.refs_12_), channel_id=1, source_target_pairs={{0,4},{4,0},{8,12},{12,8},{16,20},{20,16},{24,28},{28,24},{1,5},{5... | collective-permute-start | bytes 1548296 | tf_op jit(solution)/shard_map/gather_weights/ppermute | solution.py:702
  94.1 31.7 %collective-permute-start.15 = (bf16[2,3,128,384]{3,2,1,0:T(8,128)(2,1)S(1)}, bf16[2,3,128,384]{3,2,1,0:T(8,128)(2,1)S(1)}, u32[]{:S(2)}, u32[]{:S(2)}) collective-permute-start(bf16[2,3,128,384]{3,2,1,0:T(8,128)(2,1)S(1)} %collective-permute-done.13.refs_7_.refs_12_.refs_8_), channel_id=1, source_target_pairs={{0,4},{4,0},{8,12},{12,8},{16,20},{20,16},{24,28},{28,24},{1,5},{5... | collective-permute-start | bytes 1769480 | tf_op jit(solution)/shard_map/gather_weights/ppermute | solution.py:702
  94.6 30.0 %collective-permute-start.27 = (bf16[2,3,96,384]{3,2,1,0:T(8,128)(2,1)S(1)}, bf16[2,3,96,384]{3,2,1,0:T(8,128)(2,1)S(1)}, u32[]{:S(2)}, u32[]{:S(2)}) collective-permute-start(bf16[2,3,96,384]{3,2,1,0:T(8,128)(2,1)S(1)} %pad_maximum_fusion.5.refs_23_), channel_id=1, source_target_pairs={{0,8},{4,12},{8,0},{12,4},{16,24},{20,28},{24,16},{28,20},{1,9},{5... | collective-permute-start | bytes 1327112 | tf_op jit(solution)/shard_map/gather_weights/ppermute | solution.py:702
  124.6 35.7 %collective-permute-start.24 = (bf16[2,3,96,384]{3,2,1,0:T(8,128)(2,1)S(1)}, bf16[2,3,96,384]{3,2,1,0:T(8,128)(2,1)}, u32[]{:S(2)}, u32[]{:S(2)}) collective-permute-start(bf16[2,3,96,384]{3,2,1,0:T(8,128)(2,1)S(1)} %pad_maximum_fusion.4.refs_19_), channel_id=1, source_target_pairs={{0,4},{4,0},{8,12},{12,8},{16,20},{20,16},{24,28},{28,24},{1,5},{5... | collective-permute-start | bytes 1327112 | tf_op jit(solution)/shard_map/gather_weights/ppermute | solution.py:702
  124.7 35.6 %collective-permute-start.28 = (bf16[2,3,96,384]{3,2,1,0:T(8,128)(2,1)S(1)}, bf16[2,3,96,384]{3,2,1,0:T(8,128)(2,1)S(1)}, u32[]{:S(2)}, u32[]{:S(2)}) collective-permute-start(bf16[2,3,96,384]{3,2,1,0:T(8,128)(2,1)S(1)} %pad_maximum_fusion.5.refs_23_), channel_id=1, source_target_pairs={{0,4},{4,0},{8,12},{12,8},{16,20},{20,16},{24,28},{28,24},{1,5},{5... | collective-permute-start | bytes 1327112 | tf_op jit(solution)/shard_map/gather_weights/ppermute | solution.py:702
  125.2 35.1 %collective-permute-start.25 = (bf16[2,3,96,384]{3,2,1,0:T(8,128)(2,1)}, bf16[2,3,96,384]{3,2,1,0:T(8,128)(2,1)S(1)}, u32[]{:S(2)}, u32[]{:S(2)}) collective-permute-start(bf16[2,3,96,384]{3,2,1,0:T(8,128)(2,1)} %collective-permute-done.23.refs_20_), channel_id=1, source_target_pairs={{0,4},{4,0},{8,12},{12,8},{16,20},{20,16},{24,28},{28,24},{1,5},{5... | collective-permute-start | bytes 1327112 | tf_op jit(solution)/shard_map/gather_weights/ppermute | solution.py:702
  125.4 35.0 %collective-permute-start.29 = (bf16[2,3,96,384]{3,2,1,0:T(8,128)(2,1)S(1)}, bf16[2,3,96,384]{3,2,1,0:T(8,128)(2,1)S(1)}, u32[]{:S(2)}, u32[]{:S(2)}) collective-permute-start(bf16[2,3,96,384]{3,2,1,0:T(8,128)(2,1)S(1)} %collective-permute-done.27.refs_24_), channel_id=1, source_target_pairs={{0,4},{4,0},{8,12},{12,8},{16,20},{20,16},{24,28},{28,24},{1,5},{5... | collective-permute-start | bytes 1327112 | tf_op jit(solution)/shard_map/gather_weights/ppermute | solution.py:702
  160.1 63.6 %collective-permute-start.45 = (bf16[2,2,4,192,384]{4,3,2,1,0:T(8,128)(2,1)}, bf16[2,2,4,192,384]{4,3,2,1,0:T(8,128)(2,1)S(1)}, u32[]{:S(2)}, u32[]{:S(2)}) collective-permute-start(bf16[2,2,4,192,384]{4,3,2,1,0:T(8,128)(2,1)} %get-tuple-element.72), channel_id=1, source_target_pairs={{0,4},{4,0},{8,12},{12,8},{16,20},{20,16},{24,28},{28,24},{1,5},{5... | collective-permute-start | bytes 7077896 | tf_op jit(solution)/shard_map/reduce_down/ppermute | solution.py:702
  197.4 67.1 %collective-permute-start.40 = (bf16[2,2,4,192,384]{4,3,2,1,0:T(8,128)(2,1)}, bf16[2,2,4,192,384]{4,3,2,1,0:T(8,128)(2,1)}, u32[]{:S(2)}, u32[]{:S(2)}) collective-permute-start(bf16[2,2,4,192,384]{4,3,2,1,0:T(8,128)(2,1)} %get-tuple-element.70), channel_id=1, source_target_pairs={{0,4},{4,0},{8,12},{12,8},{16,20},{20,16},{24,28},{28,24},{1,5},{5... | collective-permute-start | bytes 7077896 | tf_op jit(solution)/shard_map/reduce_up/ppermute | solution.py:702
  225.4 35.8 %collective-permute-start.46 = (bf16[2,4,192,384]{3,2,1,0:T(8,128)(2,1)}, bf16[2,4,192,384]{3,2,1,0:T(8,128)(2,1)}, u32[]{:S(2)}, u32[]{:S(2)}) collective-permute-start(bf16[2,4,192,384]{3,2,1,0:T(8,128)(2,1)} %get-tuple-element.74), channel_id=1, source_target_pairs={{0,8},{4,12},{8,0},{12,4},{16,24},{20,28},{24,16},{28,20},{1,9},{5... | collective-permute-start | bytes 3538952 | tf_op jit(solution)/shard_map/reduce_down/ppermute | solution.py:702
  245.0 26.4 %collective-permute-start.30 = (bf16[2,2,4,160,384]{4,3,2,1,0:T(8,128)(2,1)}, bf16[2,2,4,160,384]{4,3,2,1,0:T(8,128)(2,1)}, u32[]{:S(2)}, u32[]{:S(2)}) collective-permute-start(bf16[2,2,4,160,384]{4,3,2,1,0:T(8,128)(2,1)} %get-tuple-element.66), channel_id=1, source_target_pairs={{0,4},{4,0},{8,12},{12,8},{16,20},{20,16},{24,28},{28,24},{1,5},{5... | collective-permute-start | bytes 5898248 | tf_op jit(solution)/shard_map/reduce_first/ppermute | solution.py:702
  245.0 13.6 %collective-permute-start.35 = (bf16[2,2,4,48,384]{4,3,2,1,0:T(8,128)(2,1)}, bf16[2,2,4,48,384]{4,3,2,1,0:T(8,128)(2,1)}, u32[]{:S(2)}, u32[]{:S(2)}) collective-permute-start(bf16[2,2,4,48,384]{4,3,2,1,0:T(8,128)(2,1)} %get-tuple-element.68), channel_id=1, source_target_pairs={{0,4},{4,0},{8,12},{12,8},{16,20},{20,16},{24,28},{28,24},{1,5},{5... | collective-permute-start | bytes 1769480 | tf_op jit(solution)/shard_map/reduce_out/ppermute | solution.py:702
  259.8 9.1 %collective-permute-start.36 = (bf16[2,4,48,384]{3,2,1,0:T(8,128)(2,1)S(1)}, bf16[2,4,48,384]{3,2,1,0:T(8,128)(2,1)S(1)}, u32[]{:S(2)}, u32[]{:S(2)}) collective-permute-start(bf16[2,4,48,384]{3,2,1,0:T(8,128)(2,1)S(1)} %get-tuple-element.86), channel_id=1, source_target_pairs={{0,8},{4,12},{8,0},{12,4},{16,24},{20,28},{24,16},{28,20},{1,9},{5... | collective-permute-start | bytes 884744 | tf_op jit(solution)/shard_map/reduce_out/ppermute | solution.py:702
  262.7 16.3 %collective-permute-start.47 = (bf16[4,192,384]{2,1,0:T(8,128)(2,1)S(1)}, bf16[4,192,384]{2,1,0:T(8,128)(2,1)S(1)}, u32[]{:S(2)}, u32[]{:S(2)}) collective-permute-start(bf16[4,192,384]{2,1,0:T(8,128)(2,1)S(1)} %get-tuple-element.76), channel_id=1, source_target_pairs={{0,16},{4,20},{8,24},{12,28},{16,0},{20,4},{24,8},{28,12},{1,17},{... | collective-permute-start | bytes 1769480 | tf_op jit(solution)/shard_map/reduce_down/ppermute | solution.py:702
  266.1 38.2 %collective-permute-start.41 = (bf16[2,4,192,384]{3,2,1,0:T(8,128)(2,1)S(1)}, bf16[2,4,192,384]{3,2,1,0:T(8,128)(2,1)S(1)}, u32[]{:S(2)}, u32[]{:S(2)}) collective-permute-start(bf16[2,4,192,384]{3,2,1,0:T(8,128)(2,1)S(1)} %fusion.3), channel_id=1, source_target_pairs={{0,16},{4,20},{8,24},{12,28},{16,0},{20,4},{24,8},{28,12},{1,17},{... | collective-permute-start | bytes 3538952 | tf_op jit(solution)/shard_map/reduce_up/ppermute | solution.py:702
  269.7 37.9 %collective-permute-start.37 = (bf16[4,48,384]{2,1,0:T(8,128)(2,1)}, bf16[4,48,384]{2,1,0:T(8,128)(2,1)}, u32[]{:S(2)}, u32[]{:S(2)}) collective-permute-start(bf16[4,48,384]{2,1,0:T(8,128)(2,1)} %get-tuple-element.93), channel_id=1, source_target_pairs={{0,16},{4,20},{8,24},{12,28},{16,0},{20,4},{24,8},{28,12},{1,17},{... | collective-permute-start | bytes 442376 | tf_op jit(solution)/shard_map/reduce_out/ppermute | solution.py:702
  273.8 57.8 %collective-permute-start.31 = (bf16[2,4,160,384]{3,2,1,0:T(8,128)(2,1)}, bf16[2,4,160,384]{3,2,1,0:T(8,128)(2,1)S(1)}, u32[]{:S(2)}, u32[]{:S(2)}) collective-permute-start(bf16[2,4,160,384]{3,2,1,0:T(8,128)(2,1)} %fusion.8), channel_id=1, source_target_pairs={{0,16},{4,20},{8,24},{12,28},{16,0},{20,4},{24,8},{28,12},{1,17},{... | collective-permute-start | bytes 2949128 | tf_op jit(solution)/shard_map/reduce_first/ppermute | solution.py:702
  286.7 19.5 %collective-permute-start.49 = (bf16[192,384]{1,0:T(8,128)(2,1)S(1)}, bf16[192,384]{1,0:T(8,128)(2,1)S(1)}, u32[]{:S(2)}, u32[]{:S(2)}) collective-permute-start(bf16[192,384]{1,0:T(8,128)(2,1)S(1)} %fusion.29), channel_id=1, source_target_pairs={{0,2},{1,3},{2,0},{3,1},{4,6},{5,7},{6,4},{7,5},{8,10},{9,11},{10,... | collective-permute-start | bytes 442376 | tf_op jit(solution)/shard_map/reduce_down/ppermute | solution.py:705
  305.4 26.9 %collective-permute-start.42 = (bf16[4,192,384]{2,1,0:T(8,128)(2,1)}, bf16[4,192,384]{2,1,0:T(8,128)(2,1)}, u32[]{:S(2)}, u32[]{:S(2)}) collective-permute-start(bf16[4,192,384]{2,1,0:T(8,128)(2,1)} %get-tuple-element.78), channel_id=1, source_target_pairs={{0,8},{4,12},{8,0},{12,4},{16,24},{20,28},{24,16},{28,20},{1,9},{5... | collective-permute-start | bytes 1769480 | tf_op jit(solution)/shard_map/reduce_up/ppermute | solution.py:702
  306.9 87.5 %all-gather.7.cloned.1.call-start = ((), (), s32[]{:S(2)}) async-start(), calls=%async_computation | async-start | bytes 1327104 | tf_op jit(solution)/shard_map/reduce_up/all_gather | solution.py:743
  308.6 37.2 %collective-permute-start.38 = (bf16[2,48,384]{2,1,0:T(8,128)(2,1)S(1)}, bf16[2,48,384]{2,1,0:T(8,128)(2,1)S(1)}, u32[]{:S(2)}, u32[]{:S(2)}) collective-permute-start(bf16[2,48,384]{2,1,0:T(8,128)(2,1)S(1)} %get-tuple-element.103), channel_id=1, source_target_pairs={{0,1},{1,0},{2,3},{3,2},{4,5},{5,4},{6,7},{7,6},{8,9},{9,8},{10,11... | collective-permute-start | bytes 221192 | tf_op jit(solution)/shard_map/reduce_out/ppermute | solution.py:705
  331.8 17.2 %collective-permute-start.32 = (bf16[4,160,384]{2,1,0:T(8,128)(2,1)S(1)}, bf16[4,160,384]{2,1,0:T(8,128)(2,1)S(1)}, u32[]{:S(2)}, u32[]{:S(2)}) collective-permute-start(bf16[4,160,384]{2,1,0:T(8,128)(2,1)S(1)} %get-tuple-element.80), channel_id=1, source_target_pairs={{0,8},{4,12},{8,0},{12,4},{16,24},{20,28},{24,16},{28,20},{1,9},{5... | collective-permute-start | bytes 1474568 | tf_op jit(solution)/shard_map/reduce_first/ppermute | solution.py:702
  333.6 12.4 %collective-permute-start.43 = (bf16[2,192,384]{2,1,0:T(8,128)(2,1)S(1)}, bf16[2,192,384]{2,1,0:T(8,128)(2,1)S(1)}, u32[]{:S(2)}, u32[]{:S(2)}) collective-permute-start(bf16[2,192,384]{2,1,0:T(8,128)(2,1)S(1)} %get-tuple-element.84), channel_id=1, source_target_pairs={{0,1},{1,0},{2,3},{3,2},{4,5},{5,4},{6,7},{7,6},{8,9},{9,8},{10,11... | collective-permute-start | bytes 884744 | tf_op jit(solution)/shard_map/reduce_up/ppermute | solution.py:705
  345.9 9.3 %collective-permute-start.39 = (bf16[48,384]{1,0:T(8,128)(2,1)S(1)}, bf16[48,384]{1,0:T(8,128)(2,1)S(1)}, u32[]{:S(2)}, u32[]{:S(2)}) collective-permute-start(bf16[48,384]{1,0:T(8,128)(2,1)S(1)} %fusion.38), channel_id=1, source_target_pairs={{0,2},{1,3},{2,0},{3,1},{4,6},{5,7},{6,4},{7,5},{8,10},{9,11},{10,... | collective-permute-start | bytes 110600 | tf_op jit(solution)/shard_map/reduce_out/ppermute | solution.py:705
  346.0 8.4 %collective-permute-start.44 = (bf16[192,384]{1,0:T(8,128)(2,1)S(1)}, bf16[192,384]{1,0:T(8,128)(2,1)S(1)}, u32[]{:S(2)}, u32[]{:S(2)}) collective-permute-start(bf16[192,384]{1,0:T(8,128)(2,1)S(1)} %fusion.27), channel_id=1, source_target_pairs={{0,2},{1,3},{2,0},{3,1},{4,6},{5,7},{6,4},{7,5},{8,10},{9,11},{10,... | collective-permute-start | bytes 442376 | tf_op jit(solution)/shard_map/reduce_up/ppermute | solution.py:705
  349.1 17.1 %collective-permute-start.33 = (bf16[2,160,384]{2,1,0:T(8,128)(2,1)S(1)}, bf16[2,160,384]{2,1,0:T(8,128)(2,1)S(1)}, u32[]{:S(2)}, u32[]{:S(2)}) collective-permute-start(bf16[2,160,384]{2,1,0:T(8,128)(2,1)S(1)} %get-tuple-element.88), channel_id=1, source_target_pairs={{0,1},{1,0},{2,3},{3,2},{4,5},{5,4},{6,7},{7,6},{8,9},{9,8},{10,11... | collective-permute-start | bytes 737288 | tf_op jit(solution)/shard_map/reduce_first/ppermute | solution.py:705
  366.3 8.7 %collective-permute-start.34 = (bf16[160,384]{1,0:T(8,128)(2,1)S(1)}, bf16[160,384]{1,0:T(8,128)(2,1)S(1)}, u32[]{:S(2)}, u32[]{:S(2)}) collective-permute-start(bf16[160,384]{1,0:T(8,128)(2,1)S(1)} %fusion.35), channel_id=1, source_target_pairs={{0,2},{1,3},{2,0},{3,1},{4,6},{5,7},{6,4},{7,5},{8,10},{9,11},{10,... | collective-permute-start | bytes 368648 | tf_op jit(solution)/shard_map/reduce_first/ppermute | solution.py:705
  (29 other events, 422.8 us)
Sparse Core Ops, SparseCore 0:
  307.0 26.5 all-gather.8
  355.3 24.5 all-gather.6
